TPU v7x, 256 devices: a whole 4x4x8 slice. The times are simulated.
256 devices in a mesh: gy: 16 (over z_hi, x), gz: 16 (over y, z_lo, core).
Axes of the slice: x: 4, y: 4, z: 8 (z_hi: 4, z_lo: 2; z = z_hi * 2 + z_lo), core: 2. Of those that a mesh axis runs over, the one named last changes fastest.
Arguments:
- field: bfloat16 [4, 512, 512, 512], P(None, 'gy', 'gz'), may hold values from -300 to 300
- basis_one: bfloat16 [512, 96], replicated, may hold values from -0.25 to 0.25
- basis_two: bfloat16 [512, 96], P('gy'), may hold values from -0.25 to 0.25
- basis_three: bfloat16 [512, 96], P('gz'), may hold values from -0.25 to 0.25
Outputs:
- gram_one: float32 [512, 512], P(('gy', 'gz'))
- gram_two: float32 [512, 512], P(('gy', 'gz'))
- core: float32 [4, 96, 96, 96], P(None, 'gy', 'gz')
All inputs are finite; a program needn't handle non-finite values.
Results may differ from a plain program's by a relative error of at most 0.0045.
Values may be sent and summed in bfloat16 or wider, within the bound.
No kernel may reach another device: no remote copies, remote signals or barrier semaphores. Data moves between devices by JAX's collectives and lax.ppermute only.
A program may use at most 64 MiB of HBM per device.

v0:
```python
import jax
import jax.numpy as jnp
from jax import lax
from jax.sharding import PartitionSpec as P


def shards(field, basis_one, basis_two, basis_three):
    comps, cells_two, cells_three, order_one = field.shape
    rank_size = basis_one.shape[1]
    order_two = cells_two * lax.axis_size("gy")
    order_three = cells_three * lax.axis_size("gz")
    flattened = field.reshape(-1, order_one)
    partial_one = jnp.dot(flattened.T, flattened, preferred_element_type=jnp.float32) / (
        comps * order_two * order_three
    )
    gram_one = lax.psum_scatter(partial_one, ("gy", "gz"), scatter_dimension=0, tiled=True)
    truncated = jnp.dot(flattened, basis_one, preferred_element_type=jnp.float32).astype(
        jnp.bfloat16
    )
    truncated = truncated.reshape(comps, cells_two, cells_three, rank_size)
    norm_two = 1.0 / (comps * order_three * rank_size)
    exchanged = lax.all_to_all(truncated, "gy", split_axis=2, concat_axis=1, tiled=True)
    partial_two = (
        jnp.einsum("vjkr,vmkr->jm", exchanged, exchanged, preferred_element_type=jnp.float32)
        * norm_two
    )
    gram_two = lax.psum_scatter(partial_two, ("gy", "gz"), scatter_dimension=0, tiled=True)
    wide_three = basis_three.astype(jnp.float32)
    mixed_two = jnp.einsum(
        "vjkr,js->vskr", truncated, basis_two, preferred_element_type=jnp.float32
    )
    mixed_two = lax.psum_scatter(mixed_two, "gy", scatter_dimension=1, tiled=True)
    contracted = jnp.einsum("vskr,kt->vstr", mixed_two, wide_three, precision=lax.Precision.HIGHEST)
    core = lax.psum_scatter(contracted, "gz", scatter_dimension=2, tiled=True)
    return (gram_one, gram_two, core)


def solution(mesh):
    in_specs = (P(None, "gy", "gz", None), P(), P("gy", None), P("gz", None))
    out_specs = (P(("gy", "gz"), None), P(("gy", "gz"), None), P(None, "gy", "gz", None))
    return jax.shard_map(shards, mesh=mesh, in_specs=in_specs, out_specs=out_specs, check_vma=False)
```

profile of v0, /device:TPU:2, one launch (start us, length us, event | category | flops | bytes accessed | tf_op | source)
XLA Modules:
  0.0 745.2 jit_solution(2238256219908972388)
XLA Ops:
  7.2 0.0 all-reduce.9.cloned.1.call-start
  7.2 0.8 copy-done
  8.1 3.6 convolution_convert_fusion
  11.7 0.7 copy.15
  12.3 3.7 convolution_bitcast_fusion
  16.0 8.1 %copy.22 = f32[4,96,32,96]{3,2,1,0:T(8,128)} copy(f32[4,96,32,96]{1,3,2,0:T(8,128)} %convolution_bitcast_fusion) | data formatting | bytes 9437184 | tf_op jit(solution)/shard_map/vjkr,js->vskr/transpose | solution.py:29
  24.2 1.4 copy.16
  25.6 11.5 %all-to-all-start = ((bf16[4,32,32,96]{3,1,0,2:T(8,128)(2,1)}), bf16[4,32,32,96]{3,1,0,2:T(8,128)(2,1)S(1)}, u32[]{:S(2)}, u32[]{:S(2)}) async-start(bf16[4,32,32,96]{3,1,0,2:T(8,128)(2,1)} %copy.16), calls=%async_computation | async-start | bytes 2097152 | tf_op jit(solution)/shard_map/all_to_all | solution.py:22
  37.0 0.0 all-reduce.13.cloned.1.call-start
  37.1 7.2 fusion.1
  44.3 27.7 %all-to-all-done = bf16[4,32,32,96]{3,1,0,2:T(8,128)(2,1)S(1)} async-done(((bf16[4,32,32,96]{3,1,0,2:T(8,128)(2,1)}), bf16[4,32,32,96]{3,1,0,2:T(8,128)(2,1)S(1)}, u32[]{:S(2)}, u32[]{:S(2)}) %all-to-all-start) | async-done | bytes 786464 | tf_op jit(solution)/shard_map/all_to_all | solution.py:22
  72.0 0.1 copy.18
  72.1 1.7 fusion
  73.8 0.0 all-reduce.11.cloned.1.call-start
  73.9 0.6 dynamic-slice.2
  75.1 269.1 %all-reduce.9.cloned.1.call-done = f32[4,96,32,96]{3,2,1,0:T(8,128)} async-done(((f32[4,96,32,96]{3,2,1,0:T(8,128)}), f32[4,96,32,96]{3,2,1,0:T(8,128)}) %all-reduce.9.cloned.1.call-update) | async-done | bytes 4718608
  344.2 2.1 convolution_bitcast_fusion.1
  346.3 1.4 copy.23
  347.8 0.6 dynamic-slice.4
  349.0 261.5 %all-reduce.13.cloned.1.call-done = (f32[512,512]{1,0:T(8,128)}, f32[512,512]{1,0:T(8,128)}) async-done(((f32[512,512]{1,0:T(8,128)}, f32[512,512]{1,0:T(8,128)}), (f32[512,512]{1,0:T(8,128)}, f32[512,512]{1,0:T(8,128)})) %all-reduce.13.cloned.1.call-update) | async-done | bytes 2097168
  610.5 1.3 constant_dynamic-slice_fusion.1
  611.8 125.3 %all-reduce.11.cloned.1.call-done = f32[4,6,96,96]{3,0,1,2:T(4,128)} async-done(((f32[4,6,96,96]{3,0,1,2:T(4,128)}), f32[4,6,96,96]{3,0,1,2:T(4,128)}) %all-reduce.11.cloned.1.call-update) | async-done | bytes 884752
  737.1 0.9 constant_dynamic-slice_fusion
  738.0 0.6 copy.24
  (12 shorter events, 0.1 us)
Async XLA Ops:
  7.2 0.9 copy-start
  7.2 337.1 %all-reduce.9.cloned.1.call-start = ((), (), s32[]{:S(2)}) async-start(), calls=%async_computation.1 | async-start | bytes 12582912
  8.1 4.3 copy-start.2
  25.6 46.4 %all-to-all-start = ((bf16[4,32,32,96]{3,1,0,2:T(8,128)(2,1)}), bf16[4,32,32,96]{3,1,0,2:T(8,128)(2,1)S(1)}, u32[]{:S(2)}, u32[]{:S(2)}) async-start(bf16[4,32,32,96]{3,1,0,2:T(8,128)(2,1)} %copy.16), calls=%async_computation | async-start | bytes 2097152 | tf_op jit(solution)/shard_map/all_to_all | solution.py:22
  37.0 573.4 %all-reduce.13.cloned.1.call-start = ((), (), s32[]{:S(2)}) async-start(), calls=%async_computation.3 | async-start | bytes 4194304
  44.3 29.6 %copy-start.4 = (u32[256]{0:T(256)S(1)}, u32[256]{0:T(256)}, u32[]{:S(2)}) copy-start(u32[256]{0:T(256)} %constant.13) | copy-start | bytes 3076
  44.3 300.0 %copy-start.1 = (bf16[32,96]{1,0:T(8,128)(2,1)S(1)}, bf16[32,96]{1,0:T(8,128)(2,1)}, u32[]{:S(2)}) copy-start(bf16[32,96]{1,0:T(8,128)(2,1)} %param.7) | copy-start | bytes 18436
  73.8 274.0 %copy-start.3 = (u32[256]{0:T(256)S(1)}, u32[256]{0:T(256)}, u32[]{:S(2)}) copy-start(u32[256]{0:T(256)} %constant.17) | copy-start | bytes 3076
  73.8 663.3 %all-reduce.11.cloned.1.call-start = ((), (), s32[]{:S(2)}) async-start(), calls=%async_computation.2 | async-start | bytes 2359296
Sparse Core Ops, SparseCore 0:
  24.3 319.8 all-reduce.8
  349.8 260.6 all-reduce.12
  613.1 123.9 all-reduce.10
where the time goes:
time: 746 us; the launch traced here: 745 us
  waiting for transfers between devices  684 us (92%)
  matrix products  18.3 us (2%)
  local copies, waits for them, and re-layouts  16.5 us (2%)
  between operations  15.1 us (2%)
  starting transfers between devices  11.6 us (2%)
    unnamed x6, waiting for transfers between devices  656 us
    all_to_all x1, waiting for transfers between devices, shards(): lax.all_to_all(truncated, 'gy', split_axis=2, concat_axis=1, tiled=True)  27.7 us
  transfers between devices with their start and end apart: 4, of which 4 were waited for; matrix products, arithmetic and copies ran while one was open for 2% of the time, Pallas kernels for 0%

commit v1 on v0

v1 whole, which is shorter than its diff:
```python
import jax
import jax.numpy as jnp
from jax import lax
from jax.experimental import pallas as pl
from jax.experimental.pallas import tpu as pltpu
from jax.sharding import PartitionSpec as P

F32 = jnp.float32
BF16 = jnp.bfloat16
LIMIT = 48 * 1024 * 1024


def nt_dot(a, b):
    return lax.dot_general(a, b, (((1,), (1,)), ((), ())), preferred_element_type=F32)


def truncate_kernel(b1t_ref, field_ref, out_ref, rows, tiles):
    cells = field_ref[0].reshape(1024, 512)
    trunc = nt_dot(b1t_ref[...], cells)
    for b in range(8):
        rows[pl.ds(b, 96, stride=8), :] = trunc[:, b * 128 : (b + 1) * 128]
    lane = lax.broadcasted_iota(jnp.int32, (8, 128), 1) // 32
    for block in range(24):
        part = [rows[(block * 4 + rr) * 8 : (block * 4 + rr) * 8 + 8, :] for rr in range(4)]
        for jj in range(4):
            moved = [
                part[rr] if rr == jj else pltpu.roll(part[rr], (32 * (rr - jj)) % 128, 1)
                for rr in range(4)
            ]
            low = jnp.where(lane == 0, moved[0], moved[1])
            high = jnp.where(lane == 2, moved[2], moved[3])
            tiles[pl.ds(block * 32 + jj, 8, stride=4), :] = jnp.where(lane < 2, low, high)
    out_ref[...] = tiles[...].astype(BF16).reshape(4, 6, 32, 128)


def truncate(b1t, field):
    return pl.pallas_call(
        truncate_kernel,
        out_shape=jax.ShapeDtypeStruct((16, 6, 32, 128), BF16),
        grid=(4,),
        in_specs=[
            pl.BlockSpec((96, 512), lambda v: (0, 0)),
            pl.BlockSpec((1, 32, 32, 512), lambda v: (v, 0, 0, 0)),
        ],
        out_specs=pl.BlockSpec((4, 6, 32, 128), lambda v: (v, 0, 0, 0)),
        scratch_shapes=[pltpu.VMEM((768, 128), F32), pltpu.VMEM((768, 128), F32)],
        compiler_params=pltpu.CompilerParams(vmem_limit_bytes=LIMIT),
    )(b1t, field)


def partial_kernel(whole_ref, b2t_ref, kron_ref, one_ref, out_ref, gram):
    x = jnp.concatenate([whole_ref[:, a].reshape(512, 128) for a in range(6)], axis=1)
    mixed = jnp.dot(b2t_ref[...], x, preferred_element_type=F32).astype(BF16)
    for gz in range(16):
        part = nt_dot(kron_ref[gz * 144 : (gz + 1) * 144, :], mixed)
        out_ref[gz, 256:400, :] = part.astype(BF16)

    def scatter(values, first):
        for c in range(4):
            gram[c * 512 : (c + 1) * 512, :] = values[:, c * 128 : (c + 1) * 128]
        for gz in range(16):
            for c in range(4):
                for e in range(2):
                    at = first + c * 32 + e * 16
                    rows = gram[pl.ds(c * 512 + gz * 2 + e, 16, stride=32), :]
                    out_ref[gz, at : at + 16, :] = rows.astype(BF16)

    scatter(nt_dot(x, x), 128)
    scatter(one_ref[...], 0)


def partials(whole, b2t, kron, one):
    return pl.pallas_call(
        partial_kernel,
        out_shape=jax.ShapeDtypeStruct((16, 400, 128), BF16),
        scratch_shapes=[pltpu.VMEM((2048, 128), F32)],
        compiler_params=pltpu.CompilerParams(vmem_limit_bytes=LIMIT),
    )(whole, b2t, kron, one)


def middle_kernel(in_ref, out_ref, core, cut):
    total = in_ref[0].astype(F32)
    for source in range(1, 16):
        total = total + in_ref[source].astype(F32)
    cut[...] = jnp.zeros_like(cut)
    for first in range(2):
        for c in range(4):
            for e in range(2):
                at = first * 128 + c * 32 + e * 16
                cut[pl.ds(first * 8 + e * 4 + c, 16, stride=32), :] = total[at : at + 16]
    core[0:128, :] = total[256:384].T
    tail = jnp.concatenate([total[384:400], jnp.zeros((112, 128), F32)], axis=0)
    core[128:256, :] = tail.T
    for s in range(6):
        cut[pl.ds(16 + s, 16, stride=32), :] = core[pl.ds(s, 16, stride=6), :]
        cut[pl.ds(22 + s, 16, stride=32), :] = core[pl.ds(128 + s, 16, stride=6), :]
    out_ref[...] = cut[...].astype(BF16).reshape(16, 32, 128)


def middle(received):
    return pl.pallas_call(
        middle_kernel,
        out_shape=jax.ShapeDtypeStruct((16, 32, 128), BF16),
        scratch_shapes=[pltpu.VMEM((256, 128), F32), pltpu.VMEM((512, 128), F32)],
        compiler_params=pltpu.CompilerParams(vmem_limit_bytes=LIMIT),
    )(received)


def last_kernel(scale_one, scale_two, in_ref, one_ref, two_ref, core_ref):
    total = in_ref[0, 0:16, :].astype(F32)
    for source in range(1, 16):
        total = total + in_ref[source, 0:16, :].astype(F32)
    for e in range(2):
        for c in range(4):
            lanes = slice(c * 128, (c + 1) * 128)
            one_ref[e : e + 1, lanes] = total[e * 4 + c : e * 4 + c + 1] * scale_one
            two_ref[e : e + 1, lanes] = total[8 + e * 4 + c : 9 + e * 4 + c] * scale_two
    lane = lax.broadcasted_iota(jnp.int32, (16, 128), 1)
    for v in range(4):
        blocks = [in_ref[v * 4 + g, 16:32, :].astype(F32) for g in range(4)]
        for t in range(6):
            row = jnp.zeros((16, 128), F32)
            for g in range(4):
                shift = (24 * (g - t)) % 128
                moved = pltpu.roll(blocks[g], shift, 1) if shift else blocks[g]
                if t == 5:
                    rest = jnp.concatenate([blocks[g][6:16], blocks[g][0:6]], axis=0)
                    rest = pltpu.roll(rest, 24 * g + 8, 1)
                    moved = jnp.where(lane < 24 * g + 8, moved, rest)
                row = jnp.where((lane >= 24 * g) & (lane < 24 * g + 24), moved, row)
            for s in range(6):
                core_ref[s, t, v : v + 1, :] = row[s : s + 1, 0:96]


def last(received, scale_one, scale_two):
    def body(*refs):
        last_kernel(scale_one, scale_two, *refs)

    return pl.pallas_call(
        body,
        out_shape=(
            jax.ShapeDtypeStruct((2, 512), F32),
            jax.ShapeDtypeStruct((2, 512), F32),
            jax.ShapeDtypeStruct((6, 6, 4, 96), F32),
        ),
        compiler_params=pltpu.CompilerParams(vmem_limit_bytes=LIMIT),
    )(received)


def gather_two(basis_two):
    me = lax.axis_index("gy")

    def ring(block, place, neighbour):
        got = [block]
        for step in range(1, 4):
            got.append(lax.ppermute(block, "gy", [(i, neighbour(i, step)) for i in range(16)]))
        turned = jnp.concatenate(got[::-1] + got[::-1], axis=0)
        size = block.shape[0]
        return lax.dynamic_slice_in_dim(turned, (3 - place) * size, 4 * size, axis=0)

    near = ring(basis_two, me % 4, lambda i, d: i // 4 * 4 + (i + d) % 4)
    return ring(near, me // 4, lambda i, d: (i + 4 * d) % 16)


def shards(field, basis_one, basis_two, basis_three):
    sent = truncate(basis_one.T, field)
    whole = lax.all_to_all(sent, "gy", split_axis=0, concat_axis=0, tiled=True)
    flattened = field.reshape(-1, 512)
    one = jnp.dot(flattened.T, flattened, preferred_element_type=F32)
    b2t = jnp.pad(gather_two(basis_two).T, ((0, 32), (0, 0)))
    repeated = jnp.tile(basis_three.T, (1, 24))[:, None, :]
    same = jnp.arange(24)[:, None] == jnp.arange(768)[None, :] // 32
    kron = jnp.where(same[None], repeated, jnp.zeros((), BF16)).reshape(2304, 768)
    blocks = partials(whole, b2t, kron, one)
    blocks = lax.all_to_all(blocks, "gz", split_axis=0, concat_axis=0, tiled=True)
    blocks = middle(blocks)
    blocks = lax.all_to_all(blocks, "gy", split_axis=0, concat_axis=0, tiled=True)
    gram_one, gram_two, core = last(blocks, 1.0 / 1048576, 1.0 / 196608)
    return (gram_one, gram_two, jnp.transpose(core, (2, 0, 1, 3)))


def solution(mesh):
    in_specs = (P(None, "gy", "gz", None), P(), P("gy", None), P("gz", None))
    out_specs = (P(("gy", "gz"), None), P(("gy", "gz"), None), P(None, "gy", "gz", None))
    return jax.shard_map(shards, mesh=mesh, in_specs=in_specs, out_specs=out_specs, check_vma=False)
```

time: 746 us -> 97.4 us (0.13)
  waiting for transfers between devices: 684 us -> 6.73 us
  blocking collectives: 0 us -> 42.4 us
  between operations: 15.1 us -> 0.8 us
  matrix products: 18.3 us -> 5.81 us
  local copies, waits for them, and re-layouts: 16.5 us -> 4.57 us
  starting transfers between devices: 11.6 us -> 23.1 us
  Pallas kernels: 0 us -> 10.9 us
    unnamed x6 -> x0, waiting for transfers between devices: 656 us -> none
    all_to_all x0 -> x2, blocking collectives: none -> 42.4 us  [the longest x1 27.6 us: shards(): lax.all_to_all(blocks, 'gz', split_axis=0, concat_axis=0, tiled=True)]
    all_to_all x1, waiting for transfers between devices: 27.7 us -> 0.01 us  [shards(): whole = lax.all_to_all(sent, 'gy', split_axis=0, concat_axis=0, tiled=True)]
    ppermute x0 -> x6, starting transfers between devices: none -> 13.2 us  [ring(): lax.ppermute(block, 'gy', [(i, neighbour(i, step)) for i in range(16)])]
    dot_general x5 -> x1, matrix products: 18.3 us -> 5.81 us  [shards(): one = jnp.dot(flattened.T, flattened, preferred_element_type=F32)]
    pallas_call x0 -> x4, Pallas kernels: none -> 10.9 us  [the longest x1 5.68 us: partials(): pl.pallas_call(partial_kernel, out_shape=jax.ShapeDtypeStruct((16, 400, 1...]
    transpose x2 -> x1, local copies, waits for them, and re-layouts: 9.5 us -> 0.02 us  [shards(): b2t = jnp.pad(gather_two(basis_two).T, ((0, 32), (0, 0)))]
  transfers between devices with their start and end apart: 4 -> 7, of which waited for: 4 -> 2; matrix products, arithmetic and copies ran while one was open for 2% -> 9% of each run, Pallas kernels for 0% -> 4%
where the time goes in v1:
time: 97.4 us; the launch traced here: 96.4 us
  blocking collectives  42.4 us (44%)
  starting transfers between devices  23.1 us (24%)
  Pallas kernels  10.9 us (11%)
  waiting for transfers between devices  6.73 us (7%)
  matrix products  5.81 us (6%)
  local copies, waits for them, and re-layouts  4.57 us (5%)
  other arithmetic  2 us (2%)
    all_to_all x1, blocking collectives, shards(): lax.all_to_all(blocks, 'gz', split_axis=0, concat_axis=0, tiled=True)  27.6 us
    all_to_all x1, blocking collectives, shards(): lax.all_to_all(blocks, 'gy', split_axis=0, concat_axis=0, tiled=True)  14.8 us
    ppermute x6, starting transfers between devices, ring(): lax.ppermute(block, 'gy', [(i, neighbour(i, step)) for i in range(16)])  13.2 us
    all_to_all x1, starting transfers between devices, shards(): whole = lax.all_to_all(sent, 'gy', split_axis=0, concat_axis=0, tiled=True)  9.94 us
    ppermute x6, waiting for transfers between devices, ring(): lax.ppermute(block, 'gy', [(i, neighbour(i, step)) for i in range(16)])  6.72 us
    dot_general x1, matrix products, shards(): one = jnp.dot(flattened.T, flattened, preferred_element_type=F32)  5.81 us
    pallas_call x1, Pallas kernels, partials(): pl.pallas_call(partial_kernel, out_shape=jax.ShapeDtypeStruct((16, 400, 1...  5.68 us
    pallas_call x1, Pallas kernels, truncate(): pl.pallas_call(truncate_kernel, out_shape=jax.ShapeDtypeStruct((16, 6, 32...  4.06 us
  transfers between devices with their start and end apart: 7, of which 2 were waited for; matrix products, arithmetic and copies ran while one was open for 9% of the time, Pallas kernels for 4%

profile of v1, /device:TPU:2, one launch (start us, length us, event | category | flops | bytes accessed | tf_op | source)
XLA Modules:
  0.0 96.4 jit_solution(8679971822804639528)
XLA Ops:
  0.6 0.8 copy.13
  1.4 1.6 %collective-permute-start.2 = (bf16[32,96]{0,1:T(8,128)(2,1)S(1)}, bf16[32,96]{0,1:T(8,128)(2,1)S(1)}, u32[]{:S(2)}, u32[]{:S(2)}) collective-permute-start(bf16[32,96]{0,1:T(8,128)(2,1)S(1)} %copy.13), channel_id=1, source_target_pairs={{0,16},{16,32},{32,48},{48,0},{64,80},{80,96},{96,112},{112,64},{1... | collective-permute-start | bytes 18440 | tf_op jit(solution)/shard_map/ppermute | solution.py:156
  3.0 2.8 %collective-permute-start.1 = (bf16[32,96]{0,1:T(8,128)(2,1)S(1)}, bf16[32,96]{0,1:T(8,128)(2,1)S(1)}, u32[]{:S(2)}, u32[]{:S(2)}) collective-permute-start(bf16[32,96]{0,1:T(8,128)(2,1)S(1)} %copy.13), channel_id=1, source_target_pairs={{0,32},{16,48},{32,0},{48,16},{64,96},{80,112},{96,64},{112,80},{1... | collective-permute-start | bytes 18440 | tf_op jit(solution)/shard_map/ppermute | solution.py:156
  5.8 0.4 collective-permute-start
  6.3 2.2 %copy-done = bf16[4,32,32,512]{3,2,1,0:T(8,128)(2,1)S(1)} copy-done((bf16[4,32,32,512]{3,2,1,0:T(8,128)(2,1)S(1)}, bf16[4,32,32,512]{3,2,1,0:T(8,128)(2,1)}, u32[]{:S(2)}) %copy-start) | copy-done | bytes 4194328
  8.4 0.9 copy-done.1
  9.3 4.1 %shard_map.67 = bf16[16,6,32,128]{3,2,1,0:T(8,128)(2,1)} custom-call(bf16[96,512]{1,0:T(8,128)(2,1)S(1)} %bitcast.13, bf16[4,32,32,512]{3,2,1,0:T(8,128)(2,1)S(1)} %copy-done), custom_call_target="tpu_custom_call" | custom-call | tf_op jit(solution)/shard_map/pallas_call | solution.py:37
  13.4 9.9 %all-to-all-start = ((bf16[16,6,32,128]{3,2,1,0:T(8,128)(2,1)}), bf16[16,6,32,128]{3,2,1,0:T(8,128)(2,1)S(1)}, u32[]{:S(2)}, u32[]{:S(2)}) async-start(bf16[16,6,32,128]{3,2,1,0:T(8,128)(2,1)} %shard_map.67), calls=%async_computation | async-start | bytes 1572864 | tf_op jit(solution)/shard_map/all_to_all | solution.py:167
  23.4 5.8 %convolution_bitcast_fusion.one_ref = f32[512,512]{1,0:T(8,128)S(1)} fusion(bf16[4,32,32,512]{3,2,1,0:T(8,128)(2,1)} %field_ref.1), kind=kOutput, calls=%fused_computation.1 | convolution fusion | flops 2147483648 | bytes 5242880 | tf_op jit(solution)/shard_map/dot_general | solution.py:169
  29.3 0.1 copy.18
  29.4 0.1 concatenate.6
  29.6 0.1 constant_dynamic-slice_fusion
  29.7 3.6 %collective-permute-start.3 = (bf16[128,96]{0,1:T(8,128)(2,1)S(1)}, bf16[128,96]{0,1:T(8,128)(2,1)S(1)}, u32[]{:S(2)}, u32[]{:S(2)}) collective-permute-start(bf16[128,96]{0,1:T(8,128)(2,1)S(1)} %constant_dynamic-slice_fusion), channel_id=1, source_target_pairs={{0,192},{16,208},{32,224},{48,240},{64,0},{80,16},{96,32},{112,48}... | collective-permute-start | bytes 73736 | tf_op jit(solution)/shard_map/ppermute | solution.py:156
  33.3 2.0 %broadcast_select_fusion = bf16[96,24,768]{2,1,0:T(8,128)(2,1)} fusion(pred[24,768]{1,0:T(8,128)(4,1)S(1)} %iota_compare_fusion, bf16[96,768]{1,0:T(8,128)(2,1)S(1)} %copy.18), kind=kLoop, calls=%fused_computation | loop fusion | flops 1769472 | bytes 3704832 | tf_op jit(solution)/shard_map/jit(_where)/select_n | solution.py:173
  35.3 4.7 %collective-permute-start.4 = (bf16[128,96]{0,1:T(8,128)(2,1)S(1)}, bf16[128,96]{0,1:T(8,128)(2,1)S(1)}, u32[]{:S(2)}, u32[]{:S(2)}) collective-permute-start(bf16[128,96]{0,1:T(8,128)(2,1)S(1)} %constant_dynamic-slice_fusion), channel_id=1, source_target_pairs={{0,128},{16,144},{32,160},{48,176},{64,192},{80,208},{96,224},{112... | collective-permute-start | bytes 73736 | tf_op jit(solution)/shard_map/ppermute | solution.py:156
  40.0 3.5 %collective-permute-done.3 = bf16[128,96]{0,1:T(8,128)(2,1)S(1)} collective-permute-done((bf16[128,96]{0,1:T(8,128)(2,1)S(1)}, bf16[128,96]{0,1:T(8,128)(2,1)S(1)}, u32[]{:S(2)}, u32[]{:S(2)}) %collective-permute-start.3) | collective-permute-done | bytes 24608 | tf_op jit(solution)/shard_map/ppermute | solution.py:156
  43.5 3.3 %collective-permute-done.4 = bf16[128,96]{0,1:T(8,128)(2,1)S(1)} collective-permute-done((bf16[128,96]{0,1:T(8,128)(2,1)S(1)}, bf16[128,96]{0,1:T(8,128)(2,1)S(1)}, u32[]{:S(2)}, u32[]{:S(2)}) %collective-permute-start.4) | collective-permute-done | bytes 24608 | tf_op jit(solution)/shard_map/ppermute | solution.py:156
  46.8 0.1 constant_dynamic-update-slice_fusion.4
  46.9 0.1 constant_dynamic-update-slice_fusion
  47.1 5.7 %shard_map.68 = bf16[16,400,128]{2,1,0:T(8,128)(2,1)S(1)} custom-call(bf16[16,6,32,128]{3,2,1,0:T(8,128)(2,1)S(1)} %all-to-all-done.whole_ref, bf16[128,512]{1,0:T(8,128)(2,1)S(1)} %pad.4.b2t_ref, bf16[2304,768]{1,0:T(8,128)(2,1)} %bitcast.14, f32[512,512]{1,0:T(8,128)S(1)} %convolution_bitcast_fusion.one_ref), custom_call_target="tpu_custom_call" | custom-call | tf_op jit(solution)/shard_map/pallas_call | solution.py:73
  52.7 27.6 %all_to_all.15.in_ref = bf16[16,400,128]{2,1,0:T(8,128)(2,1)S(1)} all-to-all(bf16[16,400,128]{2,1,0:T(8,128)(2,1)S(1)} %shard_map.68), channel_id=1, replica_groups=mesh['gy'=16,'gz'=16] {'gz'}, dimensions={0} | all-to-all | bytes 3276800 | tf_op jit(solution)/shard_map/all_to_all | solution.py:175
  80.4 0.4 shard_map.69
  80.8 14.8 %all_to_all.16.refs_0_ = bf16[16,32,128]{2,1,0:T(8,128)(2,1)S(1)} all-to-all(bf16[16,32,128]{2,1,0:T(8,128)(2,1)S(1)} %shard_map.69), channel_id=1, replica_groups=mesh['gy'=16,'gz'=16] {'gy'}, dimensions={0} | all-to-all | bytes 262144 | tf_op jit(solution)/shard_map/all_to_all | solution.py:177
  95.6 0.8 shard_map.70
  (21 shorter events, 0.2 us)
Async XLA Ops:
  1.4 28.0 %collective-permute-start.2 = (bf16[32,96]{0,1:T(8,128)(2,1)S(1)}, bf16[32,96]{0,1:T(8,128)(2,1)S(1)}, u32[]{:S(2)}, u32[]{:S(2)}) collective-permute-start(bf16[32,96]{0,1:T(8,128)(2,1)S(1)} %copy.13), channel_id=1, source_target_pairs={{0,16},{16,32},{32,48},{48,0},{64,80},{80,96},{96,112},{112,64},{1... | collective-permute-start | bytes 18440 | tf_op jit(solution)/shard_map/ppermute | solution.py:156
  3.0 26.4 %collective-permute-start.1 = (bf16[32,96]{0,1:T(8,128)(2,1)S(1)}, bf16[32,96]{0,1:T(8,128)(2,1)S(1)}, u32[]{:S(2)}, u32[]{:S(2)}) collective-permute-start(bf16[32,96]{0,1:T(8,128)(2,1)S(1)} %copy.13), channel_id=1, source_target_pairs={{0,32},{16,48},{32,0},{48,16},{64,96},{80,112},{96,64},{112,80},{1... | collective-permute-start | bytes 18440 | tf_op jit(solution)/shard_map/ppermute | solution.py:156
  5.8 23.6 %collective-permute-start = (bf16[32,96]{0,1:T(8,128)(2,1)S(1)}, bf16[32,96]{0,1:T(8,128)(2,1)S(1)}, u32[]{:S(2)}, u32[]{:S(2)}) collective-permute-start(bf16[32,96]{0,1:T(8,128)(2,1)S(1)} %copy.13), channel_id=1, source_target_pairs={{0,48},{16,0},{32,16},{48,32},{64,112},{80,64},{96,80},{112,96},{1... | collective-permute-start | bytes 18440 | tf_op jit(solution)/shard_map/ppermute | solution.py:156
  6.3 2.2 %copy-start = (bf16[4,32,32,512]{3,2,1,0:T(8,128)(2,1)S(1)}, bf16[4,32,32,512]{3,2,1,0:T(8,128)(2,1)}, u32[]{:S(2)}) copy-start(bf16[4,32,32,512]{3,2,1,0:T(8,128)(2,1)} %field_ref.1) | copy-start | bytes 12582916
  8.4 0.9 copy-start.1
  13.4 33.7 %all-to-all-start = ((bf16[16,6,32,128]{3,2,1,0:T(8,128)(2,1)}), bf16[16,6,32,128]{3,2,1,0:T(8,128)(2,1)S(1)}, u32[]{:S(2)}, u32[]{:S(2)}) async-start(bf16[16,6,32,128]{3,2,1,0:T(8,128)(2,1)} %shard_map.67), calls=%async_computation | async-start | bytes 1572864 | tf_op jit(solution)/shard_map/all_to_all | solution.py:167
  23.4 5.9 %copy-start.2 = (bf16[32,96]{1,0:T(8,128)(2,1)S(1)}, bf16[32,96]{1,0:T(8,128)(2,1)}, u32[]{:S(2)}) copy-start(bf16[32,96]{1,0:T(8,128)(2,1)} %param.7) | copy-start | bytes 18436
  29.7 13.8 %collective-permute-start.3 = (bf16[128,96]{0,1:T(8,128)(2,1)S(1)}, bf16[128,96]{0,1:T(8,128)(2,1)S(1)}, u32[]{:S(2)}, u32[]{:S(2)}) collective-permute-start(bf16[128,96]{0,1:T(8,128)(2,1)S(1)} %constant_dynamic-slice_fusion), channel_id=1, source_target_pairs={{0,192},{16,208},{32,224},{48,240},{64,0},{80,16},{96,32},{112,48}... | collective-permute-start | bytes 73736 | tf_op jit(solution)/shard_map/ppermute | solution.py:156
  35.3 11.5 %collective-permute-start.5 = (bf16[128,96]{0,1:T(8,128)(2,1)S(1)}, bf16[128,96]{0,1:T(8,128)(2,1)S(1)}, u32[]{:S(2)}, u32[]{:S(2)}) collective-permute-start(bf16[128,96]{0,1:T(8,128)(2,1)S(1)} %constant_dynamic-slice_fusion), channel_id=1, source_target_pairs={{0,64},{16,80},{32,96},{48,112},{64,128},{80,144},{96,160},{112,17... | collective-permute-start | bytes 73736 | tf_op jit(solution)/shard_map/ppermute | solution.py:156
  35.3 11.4 %collective-permute-start.4 = (bf16[128,96]{0,1:T(8,128)(2,1)S(1)}, bf16[128,96]{0,1:T(8,128)(2,1)S(1)}, u32[]{:S(2)}, u32[]{:S(2)}) collective-permute-start(bf16[128,96]{0,1:T(8,128)(2,1)S(1)} %constant_dynamic-slice_fusion), channel_id=1, source_target_pairs={{0,128},{16,144},{32,160},{48,176},{64,192},{80,208},{96,224},{112... | collective-permute-start | bytes 73736 | tf_op jit(solution)/shard_map/ppermute | solution.py:156

commit v2 on v0

v2 whole, which is shorter than its diff:
```python
import jax
import jax.numpy as jnp
from jax import lax
from jax.experimental import pallas as pl
from jax.experimental.pallas import tpu as pltpu
from jax.sharding import PartitionSpec as P

F32 = jnp.float32
BF16 = jnp.bfloat16
WIDE = 60 * 1024 * 1024
LIMIT = 48 * 1024 * 1024
VMEM = pl.BlockSpec(memory_space=pltpu.VMEM)
HBM = pl.BlockSpec(memory_space=pltpu.HBM)
ANY = pl.BlockSpec(memory_space=pl.ANY)


def nt_dot(a, b):
    return lax.dot_general(a, b, (((1,), (1,)), ((), ())), preferred_element_type=F32)


def call(kernel, outs, scratch=(), specs=None, limit=LIMIT, out_specs=None, name=None):
    keywords = {} if out_specs is None else {"out_specs": out_specs}
    return lambda *args: pl.pallas_call(
        kernel,
        out_shape=outs,
        in_specs=[VMEM] * len(args) if specs is None else specs,
        scratch_shapes=list(scratch),
        compiler_params=pltpu.CompilerParams(vmem_limit_bytes=limit),
        name=name,
        **keywords,
    )(*args)


def shape(dims, dtype=BF16):
    return jax.ShapeDtypeStruct(dims, dtype)


def truncate_kernel(b1t_ref, b2_ref, field_ref, out_ref, b1t, b2, b2_wide, cells, rows, tiles, sent, sems):
    core = lax.axis_index("gz") % 2
    small = [
        pltpu.make_async_copy(b1t_ref, b1t, sems.at[0]),
        pltpu.make_async_copy(b2_ref, b2, sems.at[1]),
    ]
    for copy in small:
        copy.start()
    copies = []
    for piece in range(8):
        v, half = piece // 2, pl.ds(piece % 2 * 16, 16)
        copies.append(
            pltpu.make_async_copy(field_ref.at[v, half], cells.at[v, half], sems.at[2 + piece])
        )
        copies[-1].start()
    for copy in small:
        copy.wait()
    b2_wide[...] = jnp.zeros_like(b2_wide)
    b2_wide[:, 0:96] = b2[...].astype(F32)
    share = [b2_wide[pl.ds(core * 2 + e, 8, stride=4), :] for e in range(2)]
    share = jnp.concatenate(share, axis=0).astype(BF16)
    for peer in range(16):
        sent[peer, 192:208, :] = share
    lane = lax.broadcasted_iota(jnp.int32, (8, 128), 1) // 32
    outs = []
    for v in range(4):
        for half in range(2):
            copies[v * 2 + half].wait()
            trunc = nt_dot(b1t[...], cells[v, half * 16 : half * 16 + 16].reshape(512, 512))
            for b in range(4):
                rows[pl.ds(half * 4 + b, 96, stride=8), :] = trunc[:, b * 128 : (b + 1) * 128]
        for block in range(24):
            first = block * 32
            part = [rows[first + rr * 8 : first + rr * 8 + 8, :] for rr in range(4)]
            for jj in range(4):
                moved = [
                    part[rr] if rr == jj else pltpu.roll(part[rr], (32 * (rr - jj)) % 128, 1)
                    for rr in range(4)
                ]
                low = jnp.where(lane == 0, moved[0], moved[1])
                high = jnp.where(lane == 2, moved[2], moved[3])
                tiles[first + jj * 8 : first + jj * 8 + 8, :] = jnp.where(lane < 2, low, high)
        block = slice(v * 4, v * 4 + 4)
        sent[block, 0:192, :] = tiles[...].astype(BF16).reshape(4, 192, 128)
        outs.append(pltpu.make_async_copy(sent.at[block], out_ref.at[block], sems.at[10 + v]))
        outs[-1].start()
    for copy in outs:
        copy.wait()


truncate = call(
    truncate_kernel,
    shape((16, 208, 128)),
    [
        pltpu.VMEM((96, 512), BF16),
        pltpu.VMEM((32, 96), BF16),
        pltpu.VMEM((32, 128), F32),
        pltpu.VMEM((4, 32, 32, 512), BF16),
        pltpu.VMEM((768, 128), F32),
        pltpu.VMEM((768, 128), F32),
        pltpu.VMEM((16, 208, 128), BF16),
        pltpu.SemaphoreType.DMA((14,)),
    ],
    [HBM, HBM, HBM],
    WIDE,
    HBM,
    "truncate",
)


def split_kernel(one_ref, other_ref, own_ref, gram):
    core = lax.axis_index("gz") % 2
    for c in range(4):
        gram[c * 512 : (c + 1) * 512, :] = one_ref[:, c * 128 : (c + 1) * 128]
    for out_ref, side in ((other_ref, 1 - core), (own_ref, core)):
        for b in range(8):
            for c in range(4):
                for e in range(2):
                    at = c * 32 + e * 16
                    rows = gram[pl.ds(c * 512 + b * 4 + side * 2 + e, 16, stride=32), :]
                    out_ref[b // 2, b % 2, at : at + 16, :] = rows.astype(BF16)


split = call(
    split_kernel,
    (shape((4, 2, 128, 128)), shape((4, 2, 128, 128))),
    [pltpu.VMEM((2048, 128), F32)],
    name="split",
)


def along_y_kernel(own_ref, got_ref, *out_refs):
    y = lax.axis_index("gz") // 4
    for distance, out_ref in enumerate(out_refs):
        at = lax.rem(y + distance, 4)
        out_ref[...] = (own_ref[at].astype(F32) + got_ref[at].astype(F32)).astype(BF16)


along_y = call(along_y_kernel, tuple(shape((2, 128, 128)) for _ in range(4)), name="along_y")


def along_z_kernel(*refs):
    other_ref, own_ref = refs[4:]
    place = lax.axis_index("gz") // 2 % 2
    for out_ref, at in ((other_ref, 1 - place), (own_ref, place)):
        total = refs[0][at].astype(F32)
        for ref in refs[1:4]:
            total = total + ref[at].astype(F32)
        out_ref[...] = total.astype(BF16)


along_z = call(along_z_kernel, (shape((128, 128)), shape((128, 128))), name="along_z")


def gram_kernel(whole_ref, *refs):
    other_ref, own_ref, gram = refs[-3:]
    core = lax.axis_index("gz") % 2

    def cells(first, size):
        parts = [whole_ref[:, pl.ds(a * 32 + first, size), :] for a in range(6)]
        return jnp.concatenate([part.reshape(16 * size, 128) for part in parts], axis=1)

    x = cells(0, 32)
    for out_ref, side in ((other_ref, 1 - core), (own_ref, core)):
        values = nt_dot(cells(pl.multiple_of(side * 16, 16), 16), x)
        for c in range(4):
            gram[c * 256 : (c + 1) * 256, :] = values[:, c * 128 : (c + 1) * 128]
        for b in range(8):
            for c in range(4):
                rows = gram[pl.ds(c * 256 + b, 32, stride=8), :]
                out_ref[b, c * 32 : c * 32 + 32, :] = rows.astype(BF16)


gram_part = call(
    gram_kernel,
    (shape((8, 128, 128)), shape((8, 128, 128))),
    [pltpu.VMEM((1024, 128), F32)],
    [VMEM] + [ANY] * 4,
    name="gram_part",
)


def core_kernel(whole_ref, got_ref, kron_ref, after_ref, other_ref, own_ref, basis, parts):
    core = lax.axis_index("gz") % 2
    basis[:, core] = whole_ref[:, 192:208, :]
    basis[:, 1 - core] = got_ref[...]
    x = [whole_ref[:, a * 32 : (a + 1) * 32, :].reshape(512, 128) for a in range(6)]
    mixed = lax.dot_general(
        basis[...].reshape(512, 128),
        jnp.concatenate(x, axis=1),
        (((0,), (0,)), ((), ())),
        preferred_element_type=F32,
    )
    high = mixed.astype(BF16)
    low = (mixed - high.astype(F32)).astype(BF16)
    for a in range(3):
        lanes = slice(a * 256, (a + 1) * 256)
        parts[a] = nt_dot(kron_ref[...], high[:, lanes]) + nt_dot(kron_ref[...], low[:, lanes])
    for out_ref, side in ((other_ref, 1 - core), (own_ref, core)):
        for b in range(8):
            pieces = []
            for t in range(6):
                at = pl.multiple_of((side + b * 2) * 48 + t * 8, 8)
                pieces += [parts[a, pl.ds(at, 8), :] for a in range(3)]
            out_ref[b] = jnp.concatenate(pieces, axis=0).astype(out_ref.dtype)


core_part = call(
    core_kernel,
    (shape((8, 144, 128)), shape((8, 144, 128), F32)),
    [pltpu.VMEM((16, 2, 16, 128), BF16), pltpu.VMEM((3, 768, 128), F32)],
    [VMEM, VMEM, VMEM, ANY],
    name="core_part",
)


def pair_kernel(gram_ref, gram_got_ref, core_ref, core_got_ref, out_ref):
    out_ref[:, 0:128, :] = (gram_ref[...].astype(F32) + gram_got_ref[...].astype(F32)).astype(BF16)
    out_ref[:, 128:272, :] = (core_ref[...] + core_got_ref[...].astype(F32)).astype(BF16)


pair = call(pair_kernel, shape((8, 272, 128)), name="pair")


def middle_kernel(in_ref, one_ref, one_got_ref, out_ref, sums, core, cut):
    total = in_ref[0].astype(F32)
    for source in range(1, 8):
        total = total + in_ref[source].astype(F32)
    sums[...] = total[0:128]
    cut[...] = jnp.zeros_like(cut)
    one = one_ref[...].astype(F32) + one_got_ref[...].astype(F32)
    for c in range(4):
        for e in range(2):
            at = c * 32 + e * 16
            cut[pl.ds(e * 4 + c, 16, stride=32), :] = one[at : at + 16]
            cut[pl.ds(8 + e * 4 + c, 16, stride=32), :] = sums[pl.ds(c * 32 + e, 16, stride=2), :]
    core[0:128, :] = total[128:256].T
    tail = jnp.concatenate([total[256:272], jnp.zeros((112, 128), F32)], axis=0)
    core[128:256, :] = tail.T
    for s in range(6):
        cut[pl.ds(16 + s, 16, stride=32), :] = core[pl.ds(s, 16, stride=6), :]
        cut[pl.ds(22 + s, 16, stride=32), :] = core[pl.ds(128 + s, 16, stride=6), :]
    out_ref[...] = cut[...].astype(BF16).reshape(16, 32, 128)


middle = call(
    middle_kernel,
    shape((16, 32, 128)),
    [pltpu.VMEM((128, 128), F32), pltpu.VMEM((256, 128), F32), pltpu.VMEM((512, 128), F32)],
    name="middle",
)


def last_kernel(scale_one, scale_two, in_ref, one_ref, two_ref, core_ref, turned, ordered):
    total = in_ref[0, 0:16, :].astype(F32)
    for source in range(1, 16):
        total = total + in_ref[source, 0:16, :].astype(F32)
    turned[...] = jnp.concatenate([total[8:16], jnp.zeros((120, 128), F32)], axis=0).T
    for group in range(4):
        for jj in range(4):
            rows = turned[group * 32 + jj * 8 : group * 32 + jj * 8 + 8, :]
            ordered[pl.ds(group * 32 + jj, 8, stride=4), :] = rows
    two = ordered[...].T
    for e in range(2):
        for c in range(4):
            lanes = slice(c * 128, (c + 1) * 128)
            one_ref[e : e + 1, lanes] = total[e * 4 + c : e * 4 + c + 1] * scale_one
            two_ref[e : e + 1, lanes] = two[e * 4 + c : e * 4 + c + 1] * scale_two
    lane = lax.broadcasted_iota(jnp.int32, (16, 128), 1)
    for v in range(4):
        blocks = [in_ref[v * 4 + g, 16:32, :].astype(F32) for g in range(4)]
        for t in range(6):
            row = jnp.zeros((16, 128), F32)
            for g in range(4):
                shift = (24 * (g - t)) % 128
                moved = pltpu.roll(blocks[g], shift, 1) if shift else blocks[g]
                if t == 5:
                    rest = jnp.concatenate([blocks[g][6:16], blocks[g][0:6]], axis=0)
                    rest = pltpu.roll(rest, 24 * g + 8, 1)
                    moved = jnp.where(lane < 24 * g + 8, moved, rest)
                row = jnp.where((lane >= 24 * g) & (lane < 24 * g + 24), moved, row)
            for s in range(6):
                core_ref[s, t, v : v + 1, :] = row[s : s + 1, 0:96]


def last(received, scale_one, scale_two):
    def body(*refs):
        last_kernel(scale_one, scale_two, *refs)

    outs = (shape((2, 512), F32), shape((2, 512), F32), shape((6, 6, 4, 96), F32))
    scratch = [pltpu.VMEM((128, 128), F32)] * 2
    return call(body, outs, scratch, name="last")(received)


def along_gz(y, z_lo, core):
    return [
        (i, (i // 4 + y) % 4 * 4 + (i // 2 % 2 ^ z_lo) * 2 + (i % 2 ^ core)) for i in range(16)
    ]


def send(block, y=0, z_lo=0, core=0):
    return lax.ppermute(block, "gz", along_gz(y, z_lo, core))


def shards(field, basis_one, basis_two, basis_three):
    sent = truncate(basis_one.T, basis_two, field)
    sent, field, basis_three = lax.optimization_barrier((sent, field, basis_three))
    whole = lax.all_to_all(sent, "gy", split_axis=0, concat_axis=0, tiled=True)

    flattened = field.reshape(-1, 512)
    one = jnp.dot(flattened.T, flattened, preferred_element_type=F32)
    other, own = split(one)
    blocks = along_y(own, send(other, core=1))
    blocks = [blocks[0]] + [send(blocks[d], y=d) for d in range(1, 4)]
    other, one_own = along_z(*blocks)
    one_got = send(other, z_lo=1)

    repeated = jnp.tile(basis_three.T, (1, 8))[:, None, :]
    same = jnp.arange(8)[:, None] == jnp.arange(256)[None, :] // 32
    kron = jnp.where(same[None], repeated, jnp.zeros((), BF16)).reshape(768, 256)

    basis_got = send(whole[:, 192:208], core=1)
    gram_other, gram_own = gram_part(whole, *blocks)
    gram_got = send(gram_other, core=1)
    core_other, core_own = core_part(whole, basis_got, kron, gram_other)
    core_got = send(core_other, core=1)
    summed = pair(gram_own, gram_got, core_own, core_got)
    groups = [[2 * b + core for b in range(8)] for core in range(2)]
    summed = lax.all_to_all(
        summed, "gz", split_axis=0, concat_axis=0, tiled=True, axis_index_groups=groups
    )
    cut = middle(summed, one_own, one_got)
    cut = lax.all_to_all(cut, "gy", split_axis=0, concat_axis=0, tiled=True)
    gram_one, gram_two, core = last(cut, 1.0 / 1048576, 1.0 / 196608)
    return (gram_one, gram_two, jnp.transpose(core, (2, 0, 1, 3)))


def solution(mesh):
    in_specs = (P(None, "gy", "gz", None), P(), P("gy", None), P("gz", None))
    out_specs = (P(("gy", "gz"), None), P(("gy", "gz"), None), P(None, "gy", "gz", None))
    return jax.shard_map(shards, mesh=mesh, in_specs=in_specs, out_specs=out_specs, check_vma=False)
```

time: 746 us -> 77.8 us (0.10)
  waiting for transfers between devices: 684 us -> 20.1 us
  local copies, waits for them, and re-layouts: 16.5 us -> 0.12 us
  starting transfers between devices: 11.6 us -> 26.5 us
  between operations: 15.1 us -> 0.77 us
  blocking collectives: 0 us -> 14.3 us
  matrix products: 18.3 us -> 5.82 us
  Pallas kernels: 0 us -> 9.74 us
    unnamed x6 -> x0, waiting for transfers between devices: 656 us -> none
    all_to_all x1 -> x2, waiting for transfers between devices: 27.7 us -> 9.67 us  [the longest x1 7.91 us: shards(): whole = lax.all_to_all(sent, 'gy', split_axis=0, concat_axis=0, tiled=True)]
    all_to_all x0 -> x1, blocking collectives: none -> 14.3 us  [shards(): cut = lax.all_to_all(cut, 'gy', split_axis=0, concat_axis=0, tiled=True)]
    dot_general x5 -> x1, matrix products: 18.3 us -> 5.82 us  [shards(): one = jnp.dot(flattened.T, flattened, preferred_element_type=F32)]
    ppermute x0 -> x8, waiting for transfers between devices: none -> 10.5 us  [send(): return lax.ppermute(block, 'gz', along_gz(y, z_lo, core))]
    pallas_call x0 -> x9, Pallas kernels: none -> 9.74 us  [call(): pl.pallas_call(kernel, out_shape=outs, in_specs=[VMEM] * len(args) if spe...]
    transpose x2 -> x0, local copies, waits for them, and re-layouts: 9.5 us -> none  [the longest x1 8.11 us: shards(): jnp.einsum('vjkr,js->vskr', truncated, basis_two, preferred_element_type=...]
    ppermute x0 -> x8, starting transfers between devices: none -> 8.7 us  [send(): return lax.ppermute(block, 'gz', along_gz(y, z_lo, core))]
  transfers between devices with their start and end apart: 4 -> 10, of which waited for: 4 -> 6; matrix products, arithmetic and copies ran while one was open for 2% -> 8% of each run, Pallas kernels for 0% -> 2%
where the time goes in v2:
time: 77.8 us; the launch traced here: 77.5 us
  starting transfers between devices  26.5 us (34%)
  waiting for transfers between devices  20.1 us (26%)
  blocking collectives  14.3 us (18%)
  Pallas kernels  9.74 us (13%)
  matrix products  5.82 us (7%)
    all_to_all x1, blocking collectives, shards(): cut = lax.all_to_all(cut, 'gy', split_axis=0, concat_axis=0, tiled=True)  14.3 us
    all_to_all x1, starting transfers between devices, shards(): whole = lax.all_to_all(sent, 'gy', split_axis=0, concat_axis=0, tiled=True)  11.5 us
    ppermute x8, waiting for transfers between devices, send(): return lax.ppermute(block, 'gz', along_gz(y, z_lo, core))  10.5 us
    pallas_call x9, Pallas kernels, call(): pl.pallas_call(kernel, out_shape=outs, in_specs=[VMEM] * len(args) if spe...  9.74 us
    ppermute x8, starting transfers between devices, send(): return lax.ppermute(block, 'gz', along_gz(y, z_lo, core))  8.7 us
    all_to_all x1, waiting for transfers between devices, shards(): whole = lax.all_to_all(sent, 'gy', split_axis=0, concat_axis=0, tiled=True)  7.91 us
    all_to_all x1, starting transfers between devices, shards(): lax.all_to_all(summed, 'gz', split_axis=0, concat_axis=0, tiled=True, axi...  6.35 us
    dot_general x1, matrix products, shards(): one = jnp.dot(flattened.T, flattened, preferred_element_type=F32)  5.82 us
  transfers between devices with their start and end apart: 10, of which 6 were waited for; matrix products, arithmetic and copies ran while one was open for 8% of the time, Pallas kernels for 2%

profile of v2, /device:TPU:2, one launch (start us, length us, event | category | flops | bytes accessed | tf_op | source)
XLA Modules:
  0.0 77.5 jit_solution(16815751646955166831)
XLA Ops:
  0.6 5.1 %truncate.1 = bf16[16,208,128]{2,1,0:T(8,128)(2,1)} custom-call(bf16[96,512]{1,0:T(8,128)(2,1)} %bitcast.13, bf16[32,96]{1,0:T(8,128)(2,1)} %b2_ref.1, bf16[4,32,32,512]{3,2,1,0:T(8,128)(2,1)} %field_ref.1), custom_call_target="tpu_custom_call" | custom-call | tf_op jit(solution)/shard_map/truncate/pallas_call | solution.py:23
  5.7 11.5 %all-to-all-start = ((bf16[16,208,128]{2,1,0:T(8,128)(2,1)}), bf16[16,208,128]{2,1,0:T(8,128)(2,1)S(1)}, u32[]{:S(2)}, u32[]{:S(2)}) async-start(bf16[16,208,128]{2,1,0:T(8,128)(2,1)} %truncate.1), calls=%async_computation | async-start | bytes 1703936 | tf_op jit(solution)/shard_map/all_to_all | solution.py:305
  17.2 5.8 %convolution_bitcast_fusion.one_ref = f32[512,512]{1,0:T(8,128)S(1)} fusion(bf16[4,32,32,512]{3,2,1,0:T(8,128)(2,1)} %field_ref.1), kind=kOutput, calls=%fused_computation | convolution fusion | flops 2147483648 | bytes 5242880 | tf_op jit(solution)/shard_map/dot_general | solution.py:308
  23.0 0.6 split.1
  23.8 0.1 copy.8
  24.0 1.4 %collective-permute-done.got_ref = bf16[4,2,128,128]{3,2,1,0:T(8,128)(2,1)S(1)} collective-permute-done((bf16[4,2,128,128]{3,2,1,0:T(8,128)(2,1)S(1)}, bf16[4,2,128,128]{3,2,1,0:T(8,128)(2,1)S(1)}, u32[]{:S(2)}, u32[]{:S(2)}) %collective-permute-start) | collective-permute-done | bytes 262176 | tf_op jit(solution)/shard_map/ppermute | solution.py:299
  25.4 1.7 %collective-permute-start.1 = (bf16[2,128,128]{2,1,0:T(8,128)(2,1)S(1)}, bf16[2,128,128]{2,1,0:T(8,128)(2,1)S(1)}, u32[]{:S(2)}, u32[]{:S(2)}) collective-permute-start(bf16[2,128,128]{2,1,0:T(8,128)(2,1)S(1)} %get-tuple-element.26), channel_id=1, source_target_pairs={{0,4},{1,5},{2,6},{3,7},{4,8},{5,9},{6,10},{7,11},{8,12},{9,13},{1... | collective-permute-start | bytes 196616 | tf_op jit(solution)/shard_map/ppermute | solution.py:299
  27.0 2.9 %collective-permute-start.2 = (bf16[2,128,128]{2,1,0:T(8,128)(2,1)S(1)}, bf16[2,128,128]{2,1,0:T(8,128)(2,1)S(1)}, u32[]{:S(2)}, u32[]{:S(2)}) collective-permute-start(bf16[2,128,128]{2,1,0:T(8,128)(2,1)S(1)} %get-tuple-element.27), channel_id=1, source_target_pairs={{0,8},{1,9},{2,10},{3,11},{4,12},{5,13},{6,14},{7,15},{8,0},{9,1},... | collective-permute-start | bytes 196616 | tf_op jit(solution)/shard_map/ppermute | solution.py:299
  29.9 1.3 %collective-permute-start.3 = (bf16[2,128,128]{2,1,0:T(8,128)(2,1)S(1)}, bf16[2,128,128]{2,1,0:T(8,128)(2,1)S(1)}, u32[]{:S(2)}, u32[]{:S(2)}) collective-permute-start(bf16[2,128,128]{2,1,0:T(8,128)(2,1)S(1)} %get-tuple-element.28), channel_id=1, source_target_pairs={{0,12},{1,13},{2,14},{3,15},{4,0},{5,1},{6,2},{7,3},{8,4},{9,5},{1... | collective-permute-start | bytes 196616 | tf_op jit(solution)/shard_map/ppermute | solution.py:299
  31.3 7.9 %all-to-all-done.whole_ref = bf16[16,208,128]{2,1,0:T(8,128)(2,1)S(1)} async-done(((bf16[16,208,128]{2,1,0:T(8,128)(2,1)}), bf16[16,208,128]{2,1,0:T(8,128)(2,1)S(1)}, u32[]{:S(2)}, u32[]{:S(2)}) %all-to-all-start) | async-done | bytes 852000 | tf_op jit(solution)/shard_map/all_to_all | solution.py:305
  39.3 0.7 gram_part.1
  40.0 0.5 collective-permute-done.5.got_ref
  40.5 1.2 %core_part.1 = (bf16[8,144,128]{2,1,0:T(8,128)(2,1)S(1)}, f32[8,144,128]{2,1,0:T(8,128)S(1)}) custom-call(bf16[16,208,128]{2,1,0:T(8,128)(2,1)S(1)} %all-to-all-done.whole_ref, bf16[16,16,128]{2,1,0:T(8,128)(2,1)S(1)} %collective-permute-done.5.got_ref, bf16[768,256]{1,0:T(8,128)(2,1)S(1)} %select_bitcast_fusion.kron_ref, ...), custom_call_target="tpu_custom_call" | custom-call | tf_op jit(solution)/shard_map/core_part/pallas_call | solution.py:23
  41.6 0.2 collective-permute-start.6
  41.9 0.4 collective-permute-start.4
  42.2 1.4 %collective-permute-done.4.gram_got_ref = bf16[8,128,128]{2,1,0:T(8,128)(2,1)S(1)} collective-permute-done((bf16[8,128,128]{2,1,0:T(8,128)(2,1)S(1)}, bf16[8,128,128]{2,1,0:T(8,128)(2,1)S(1)}, u32[]{:S(2)}, u32[]{:S(2)}) %collective-permute-start.4) | collective-permute-done | bytes 262176 | tf_op jit(solution)/shard_map/ppermute | solution.py:299
  43.7 0.9 %pair.1 = bf16[8,272,128]{2,1,0:T(8,128)(2,1)} custom-call(bf16[8,128,128]{2,1,0:T(8,128)(2,1)S(1)} %get-tuple-element.29.gram_ref, bf16[8,128,128]{2,1,0:T(8,128)(2,1)S(1)} %collective-permute-done.4.gram_got_ref, f32[8,144,128]{2,1,0:T(8,128)S(1)} %get-tuple-element.32.core_ref, bf16[8,144,128]{2,1,0:T(8,128)(2,1)S(1)} %collective-permute-done.6.core_got_ref), custom_call_target="tpu_custom_call" | custom-call | tf_op jit(solution)/shard_map/pair/pallas_call | solution.py:23
  44.6 6.4 %all-to-all-start.1 = ((bf16[8,272,128]{2,1,0:T(8,128)(2,1)}), bf16[8,272,128]{2,1,0:T(8,128)(2,1)S(1)}, u32[]{:S(2)}, u32[]{:S(2)}) async-start(bf16[8,272,128]{2,1,0:T(8,128)(2,1)} %pair.1), calls=%async_computation.1 | async-start | bytes 1114112 | tf_op jit(solution)/shard_map/all_to_all | solution.py:326
  51.0 2.1 %collective-permute-start.7 = (bf16[128,128]{1,0:T(8,128)(2,1)S(1)}, bf16[128,128]{1,0:T(8,128)(2,1)S(1)}, u32[]{:S(2)}, u32[]{:S(2)}) collective-permute-start(bf16[128,128]{1,0:T(8,128)(2,1)S(1)} %get-tuple-element.35), channel_id=1, source_target_pairs={{0,2},{1,3},{2,0},{3,1},{4,6},{5,7},{6,4},{7,5},{8,10},{9,11},{10,... | collective-permute-start | bytes 98312 | tf_op jit(solution)/shard_map/ppermute | solution.py:299
  53.1 7.2 %collective-permute-done.7.one_got_ref = bf16[128,128]{1,0:T(8,128)(2,1)S(1)} collective-permute-done((bf16[128,128]{1,0:T(8,128)(2,1)S(1)}, bf16[128,128]{1,0:T(8,128)(2,1)S(1)}, u32[]{:S(2)}, u32[]{:S(2)}) %collective-permute-start.7) | collective-permute-done | bytes 32800 | tf_op jit(solution)/shard_map/ppermute | solution.py:299
  60.3 1.8 %all-to-all-done.1.in_ref = bf16[8,272,128]{2,1,0:T(8,128)(2,1)S(1)} async-done(((bf16[8,272,128]{2,1,0:T(8,128)(2,1)}), bf16[8,272,128]{2,1,0:T(8,128)(2,1)S(1)}, u32[]{:S(2)}, u32[]{:S(2)}) %all-to-all-start.1) | async-done | bytes 557088 | tf_op jit(solution)/shard_map/all_to_all | solution.py:326
  62.1 0.3 middle.1
  62.3 14.3 %all_to_all.15.refs_0_ = bf16[16,32,128]{2,1,0:T(8,128)(2,1)S(1)} all-to-all(bf16[16,32,128]{2,1,0:T(8,128)(2,1)S(1)} %middle.1), channel_id=1, replica_groups=mesh['gy'=16,'gz'=16] {'gy'}, dimensions={0} | all-to-all | bytes 262144 | tf_op jit(solution)/shard_map/all_to_all | solution.py:330
  76.6 0.9 %last.1 = (f32[2,512]{1,0:T(2,128)}, f32[2,512]{1,0:T(2,128)}, f32[6,6,4,96]{3,2,1,0:T(4,128)}) custom-call(bf16[16,32,128]{2,1,0:T(8,128)(2,1)S(1)} %all_to_all.15.refs_0_), custom_call_target="tpu_custom_call" | custom-call | tf_op jit(solution)/shard_map/last/pallas_call | solution.py:23
  (15 shorter events, 0.3 us)
Async XLA Ops:
  5.7 33.5 %all-to-all-start = ((bf16[16,208,128]{2,1,0:T(8,128)(2,1)}), bf16[16,208,128]{2,1,0:T(8,128)(2,1)S(1)}, u32[]{:S(2)}, u32[]{:S(2)}) async-start(bf16[16,208,128]{2,1,0:T(8,128)(2,1)} %truncate.1), calls=%async_computation | async-start | bytes 1703936 | tf_op jit(solution)/shard_map/all_to_all | solution.py:305
  17.2 6.6 %copy-start = (bf16[32,96]{1,0:T(8,128)(2,1)S(1)}, bf16[32,96]{1,0:T(8,128)(2,1)}, u32[]{:S(2)}) copy-start(bf16[32,96]{1,0:T(8,128)(2,1)} %param.7) | copy-start | bytes 18436
  23.7 1.6 %collective-permute-start = (bf16[4,2,128,128]{3,2,1,0:T(8,128)(2,1)S(1)}, bf16[4,2,128,128]{3,2,1,0:T(8,128)(2,1)S(1)}, u32[]{:S(2)}, u32[]{:S(2)}) collective-permute-start(bf16[4,2,128,128]{3,2,1,0:T(8,128)(2,1)S(1)} %get-tuple-element.24), channel_id=1, source_target_pairs={{0,1},{1,0},{2,3},{3,2},{4,5},{5,4},{6,7},{7,6},{8,9},{9,8},{10,11... | collective-permute-start | bytes 786440 | tf_op jit(solution)/shard_map/ppermute | solution.py:299
  25.4 13.9 %collective-permute-start.1 = (bf16[2,128,128]{2,1,0:T(8,128)(2,1)S(1)}, bf16[2,128,128]{2,1,0:T(8,128)(2,1)S(1)}, u32[]{:S(2)}, u32[]{:S(2)}) collective-permute-start(bf16[2,128,128]{2,1,0:T(8,128)(2,1)S(1)} %get-tuple-element.26), channel_id=1, source_target_pairs={{0,4},{1,5},{2,6},{3,7},{4,8},{5,9},{6,10},{7,11},{8,12},{9,13},{1... | collective-permute-start | bytes 196616 | tf_op jit(solution)/shard_map/ppermute | solution.py:299
  27.0 12.3 %collective-permute-start.2 = (bf16[2,128,128]{2,1,0:T(8,128)(2,1)S(1)}, bf16[2,128,128]{2,1,0:T(8,128)(2,1)S(1)}, u32[]{:S(2)}, u32[]{:S(2)}) collective-permute-start(bf16[2,128,128]{2,1,0:T(8,128)(2,1)S(1)} %get-tuple-element.27), channel_id=1, source_target_pairs={{0,8},{1,9},{2,10},{3,11},{4,12},{5,13},{6,14},{7,15},{8,0},{9,1},... | collective-permute-start | bytes 196616 | tf_op jit(solution)/shard_map/ppermute | solution.py:299
  29.9 9.4 %collective-permute-start.3 = (bf16[2,128,128]{2,1,0:T(8,128)(2,1)S(1)}, bf16[2,128,128]{2,1,0:T(8,128)(2,1)S(1)}, u32[]{:S(2)}, u32[]{:S(2)}) collective-permute-start(bf16[2,128,128]{2,1,0:T(8,128)(2,1)S(1)} %get-tuple-element.28), channel_id=1, source_target_pairs={{0,12},{1,13},{2,14},{3,15},{4,0},{5,1},{6,2},{7,3},{8,4},{9,5},{1... | collective-permute-start | bytes 196616 | tf_op jit(solution)/shard_map/ppermute | solution.py:299
  39.2 1.3 %collective-permute-start.5 = (bf16[16,16,128]{2,1,0:T(8,128)(2,1)S(1)}, bf16[16,16,128]{2,1,0:T(8,128)(2,1)S(1)}, u32[]{:S(2)}, u32[]{:S(2)}) collective-permute-start(bf16[16,16,128]{2,1,0:T(8,128)(2,1)S(1)} %slice.4), channel_id=1, source_target_pairs={{0,1},{1,0},{2,3},{3,2},{4,5},{5,4},{6,7},{7,6},{8,9},{9,8},{10,11... | collective-permute-start | bytes 196616 | tf_op jit(solution)/shard_map/ppermute | solution.py:299
  41.6 2.0 %collective-permute-start.6 = (bf16[8,144,128]{2,1,0:T(8,128)(2,1)S(1)}, bf16[8,144,128]{2,1,0:T(8,128)(2,1)S(1)}, u32[]{:S(2)}, u32[]{:S(2)}) collective-permute-start(bf16[8,144,128]{2,1,0:T(8,128)(2,1)S(1)} %get-tuple-element.33), channel_id=1, source_target_pairs={{0,1},{1,0},{2,3},{3,2},{4,5},{5,4},{6,7},{7,6},{8,9},{9,8},{10,11... | collective-permute-start | bytes 884744 | tf_op jit(solution)/shard_map/ppermute | solution.py:299
  41.9 1.8 %collective-permute-start.4 = (bf16[8,128,128]{2,1,0:T(8,128)(2,1)S(1)}, bf16[8,128,128]{2,1,0:T(8,128)(2,1)S(1)}, u32[]{:S(2)}, u32[]{:S(2)}) collective-permute-start(bf16[8,128,128]{2,1,0:T(8,128)(2,1)S(1)} %get-tuple-element.30.after_ref), channel_id=1, source_target_pairs={{0,1},{1,0},{2,3},{3,2},{4,5},{5,4},{6,7},{7,6},{8,9},{9,8},{10,11... | collective-permute-start | bytes 786440 | tf_op jit(solution)/shard_map/ppermute | solution.py:299
  44.6 17.5 %all-to-all-start.1 = ((bf16[8,272,128]{2,1,0:T(8,128)(2,1)}), bf16[8,272,128]{2,1,0:T(8,128)(2,1)S(1)}, u32[]{:S(2)}, u32[]{:S(2)}) async-start(bf16[8,272,128]{2,1,0:T(8,128)(2,1)} %pair.1), calls=%async_computation.1 | async-start | bytes 1114112 | tf_op jit(solution)/shard_map/all_to_all | solution.py:326
  51.0 9.3 %collective-permute-start.7 = (bf16[128,128]{1,0:T(8,128)(2,1)S(1)}, bf16[128,128]{1,0:T(8,128)(2,1)S(1)}, u32[]{:S(2)}, u32[]{:S(2)}) collective-permute-start(bf16[128,128]{1,0:T(8,128)(2,1)S(1)} %get-tuple-element.35), channel_id=1, source_target_pairs={{0,2},{1,3},{2,0},{3,1},{4,6},{5,7},{6,4},{7,5},{8,10},{9,11},{10,... | collective-permute-start | bytes 98312 | tf_op jit(solution)/shard_map/ppermute | solution.py:299

commit v3 on v2

--- a/solution.py
+++ b/solution.py
@@ -1,3 +1,5 @@
+import functools
+
 import jax
 import jax.numpy as jnp
 from jax import lax
@@ -61,11 +63,11 @@
     lane = lax.broadcasted_iota(jnp.int32, (8, 128), 1) // 32
     outs = []
     for v in range(4):
-        for half in range(2):
-            copies[v * 2 + half].wait()
-            trunc = nt_dot(b1t[...], cells[v, half * 16 : half * 16 + 16].reshape(512, 512))
-            for b in range(4):
-                rows[pl.ds(half * 4 + b, 96, stride=8), :] = trunc[:, b * 128 : (b + 1) * 128]
+        for copy in copies[v * 2 : v * 2 + 2]:
+            copy.wait()
+        trunc = nt_dot(b1t[...], cells[v].reshape(1024, 512))
+        for b in range(8):
+            rows[pl.ds(b, 96, stride=8), :] = trunc[:, b * 128 : (b + 1) * 128]
         for block in range(24):
             first = block * 32
             part = [rows[first + rr * 8 : first + rr * 8 + 8, :] for rr in range(4)]
@@ -149,35 +151,46 @@
 along_z = call(along_z_kernel, (shape((128, 128)), shape((128, 128))), name="along_z")
 
 
-def gram_kernel(whole_ref, *refs):
-    other_ref, own_ref, gram = refs[-3:]
-    core = lax.axis_index("gz") % 2
+def gram_kernel(away, whole_ref, *refs):
+    out_ref, gram = refs[-2:]
+    side = (lax.axis_index("gz") + away) % 2
 
     def cells(first, size):
         parts = [whole_ref[:, pl.ds(a * 32 + first, size), :] for a in range(6)]
         return jnp.concatenate([part.reshape(16 * size, 128) for part in parts], axis=1)
 
-    x = cells(0, 32)
-    for out_ref, side in ((other_ref, 1 - core), (own_ref, core)):
-        values = nt_dot(cells(pl.multiple_of(side * 16, 16), 16), x)
+    values = nt_dot(cells(pl.multiple_of(side * 16, 16), 16), cells(0, 32))
+    for c in range(4):
+        gram[c * 256 : (c + 1) * 256, :] = values[:, c * 128 : (c + 1) * 128]
+    for b in range(8):
         for c in range(4):
-            gram[c * 256 : (c + 1) * 256, :] = values[:, c * 128 : (c + 1) * 128]
-        for b in range(8):
-            for c in range(4):
-                rows = gram[pl.ds(c * 256 + b, 32, stride=8), :]
-                out_ref[b, c * 32 : c * 32 + 32, :] = rows.astype(BF16)
-
-
-gram_part = call(
-    gram_kernel,
-    (shape((8, 128, 128)), shape((8, 128, 128))),
-    [pltpu.VMEM((1024, 128), F32)],
-    [VMEM] + [ANY] * 4,
-    name="gram_part",
-)
-
-
-def core_kernel(whole_ref, got_ref, kron_ref, after_ref, other_ref, own_ref, basis, parts):
+            rows = gram[pl.ds(c * 256 + b, 32, stride=8), :]
+            out_ref[b, c * 32 : c * 32 + 32, :] = rows.astype(BF16)
+
+
+def gram_part(away, whole, *after):
+    return call(
+        functools.partial(gram_kernel, away),
+        shape((8, 128, 128)),
+        [pltpu.VMEM((1024, 128), F32)],
+        [VMEM] + [ANY] * len(after),
+        name="gram_other" if away else "gram_own",
+    )(whole, *after)
+
+
+def core_rows(parts_ref, b, side):
+    pieces = []
+    for t in range(6):
+        at = pl.multiple_of((side + b * 2) * 48 + t * 8, 8)
+        pieces += [parts_ref[a, pl.ds(at, 8), :] for a in range(3)]
+    rest = jnp.concatenate(pieces[14:], axis=0)
+    rest = [pltpu.roll(rest, 96 - 32 * g, 1) for g in range(3)]
+    rest = jnp.concatenate(rest + [jnp.zeros((16, 128), F32)], axis=0)
+    lane = lax.broadcasted_iota(jnp.int32, (112, 128), 1)
+    return jnp.where(lane < 96, jnp.concatenate(pieces[:14], axis=0), rest)
+
+
+def core_kernel(whole_ref, got_ref, kron_ref, after_ref, other_ref, parts_ref, basis):
     core = lax.axis_index("gz") % 2
     basis[:, core] = whole_ref[:, 192:208, :]
     basis[:, 1 - core] = got_ref[...]
@@ -192,31 +205,29 @@
     low = (mixed - high.astype(F32)).astype(BF16)
     for a in range(3):
         lanes = slice(a * 256, (a + 1) * 256)
-        parts[a] = nt_dot(kron_ref[...], high[:, lanes]) + nt_dot(kron_ref[...], low[:, lanes])
-    for out_ref, side in ((other_ref, 1 - core), (own_ref, core)):
-        for b in range(8):
-            pieces = []
-            for t in range(6):
-                at = pl.multiple_of((side + b * 2) * 48 + t * 8, 8)
-                pieces += [parts[a, pl.ds(at, 8), :] for a in range(3)]
-            out_ref[b] = jnp.concatenate(pieces, axis=0).astype(out_ref.dtype)
+        parts_ref[a] = nt_dot(kron_ref[...], high[:, lanes]) + nt_dot(kron_ref[...], low[:, lanes])
+    for b in range(8):
+        other_ref[b] = core_rows(parts_ref, b, 1 - core).astype(BF16)
 
 
 core_part = call(
     core_kernel,
-    (shape((8, 144, 128)), shape((8, 144, 128), F32)),
-    [pltpu.VMEM((16, 2, 16, 128), BF16), pltpu.VMEM((3, 768, 128), F32)],
+    (shape((8, 112, 128)), shape((3, 768, 128), F32)),
+    [pltpu.VMEM((16, 2, 16, 128), BF16)],
     [VMEM, VMEM, VMEM, ANY],
     name="core_part",
 )
 
 
-def pair_kernel(gram_ref, gram_got_ref, core_ref, core_got_ref, out_ref):
+def pair_kernel(gram_ref, gram_got_ref, parts_ref, core_got_ref, out_ref):
+    core = lax.axis_index("gz") % 2
     out_ref[:, 0:128, :] = (gram_ref[...].astype(F32) + gram_got_ref[...].astype(F32)).astype(BF16)
-    out_ref[:, 128:272, :] = (core_ref[...] + core_got_ref[...].astype(F32)).astype(BF16)
-
-
-pair = call(pair_kernel, shape((8, 272, 128)), name="pair")
+    for b in range(8):
+        total = core_rows(parts_ref, b, core) + core_got_ref[b].astype(F32)
+        out_ref[b, 128:240, :] = total.astype(BF16)
+
+
+pair = call(pair_kernel, shape((8, 240, 128)), name="pair")
 
 
 def middle_kernel(in_ref, one_ref, one_got_ref, out_ref, sums, core, cut):
@@ -231,8 +242,11 @@
             at = c * 32 + e * 16
             cut[pl.ds(e * 4 + c, 16, stride=32), :] = one[at : at + 16]
             cut[pl.ds(8 + e * 4 + c, 16, stride=32), :] = sums[pl.ds(c * 32 + e, 16, stride=2), :]
-    core[0:128, :] = total[128:256].T
-    tail = jnp.concatenate([total[256:272], jnp.zeros((112, 128), F32)], axis=0)
+    rest = [pltpu.roll(total[128 + g * 32 : 160 + g * 32], (32 + 32 * g) % 128, 1) for g in range(3)]
+    lane = lax.broadcasted_iota(jnp.int32, (32, 128), 1)
+    rest = jnp.where(lane < 32, rest[0], jnp.where(lane < 64, rest[1], rest[2]))
+    core[0:128, :] = jnp.concatenate([total[128:240], rest[0:16]], axis=0).T
+    tail = jnp.concatenate([rest[16:32], jnp.zeros((112, 128), F32)], axis=0)
     core[128:256, :] = tail.T
     for s in range(6):
         cut[pl.ds(16 + s, 16, stride=32), :] = core[pl.ds(s, 16, stride=6), :]
@@ -248,7 +262,7 @@
 )
 
 
-def last_kernel(scale_one, scale_two, in_ref, one_ref, two_ref, core_ref, turned, ordered):
+def last_kernel(scale_one, scale_two, in_ref, one_ref, two_ref, core_ref, turned, ordered, core):
     total = in_ref[0, 0:16, :].astype(F32)
     for source in range(1, 16):
         total = total + in_ref[source, 0:16, :].astype(F32)
@@ -276,8 +290,10 @@
                     rest = pltpu.roll(rest, 24 * g + 8, 1)
                     moved = jnp.where(lane < 24 * g + 8, moved, rest)
                 row = jnp.where((lane >= 24 * g) & (lane < 24 * g + 24), moved, row)
-            for s in range(6):
-                core_ref[s, t, v : v + 1, :] = row[s : s + 1, 0:96]
+            core[pl.ds(t * 4 + v, 8, stride=24), :] = row[0:8]
+    for s in range(6):
+        for t in range(6):
+            core_ref[s, t] = core[(s * 6 + t) * 4 : (s * 6 + t) * 4 + 4, 0:96]
 
 
 def last(received, scale_one, scale_two):
@@ -285,7 +301,7 @@
         last_kernel(scale_one, scale_two, *refs)
 
     outs = (shape((2, 512), F32), shape((2, 512), F32), shape((6, 6, 4, 96), F32))
-    scratch = [pltpu.VMEM((128, 128), F32)] * 2
+    scratch = [pltpu.VMEM((rows, 128), F32) for rows in (128, 128, 192)]
     return call(body, outs, scratch, name="last")(received)
 
 
@@ -317,11 +333,12 @@
     kron = jnp.where(same[None], repeated, jnp.zeros((), BF16)).reshape(768, 256)
 
     basis_got = send(whole[:, 192:208], core=1)
-    gram_other, gram_own = gram_part(whole, *blocks)
+    gram_other = gram_part(1, whole, one_own, one_got)
     gram_got = send(gram_other, core=1)
-    core_other, core_own = core_part(whole, basis_got, kron, gram_other)
+    core_other, core_parts = core_part(whole, basis_got, kron, gram_other)
     core_got = send(core_other, core=1)
-    summed = pair(gram_own, gram_got, core_own, core_got)
+    gram_own = gram_part(0, whole, core_other)
+    summed = pair(gram_own, gram_got, core_parts, core_got)
     groups = [[2 * b + core for b in range(8)] for core in range(2)]
     summed = lax.all_to_all(
         summed, "gz", split_axis=0, concat_axis=0, tiled=True, axis_index_groups=groups

time: 77.8 us -> 75.7 us (0.973)
  blocking collectives: 14.3 us -> 31.2 us
  waiting for transfers between devices: 20.1 us -> 9.15 us
  starting transfers between devices: 26.5 us -> 19.4 us
  Pallas kernels: 9.74 us -> 8.93 us
    all_to_all x0 -> x1, blocking collectives: none -> 16.3 us  [shards(): lax.all_to_all(summed, 'gz', split_axis=0, concat_axis=0, tiled=True, axi...]
    all_to_all x1 -> x0, starting transfers between devices: 6.35 us -> none  [shards(): lax.all_to_all(summed, 'gz', split_axis=0, concat_axis=0, tiled=True, axi...]
    ppermute x8, waiting for transfers between devices: 10.5 us -> 5.44 us  [send(): return lax.ppermute(block, 'gz', along_gz(y, z_lo, core))]
    all_to_all x1, waiting for transfers between devices: 7.91 us -> 3.72 us  [shards(): whole = lax.all_to_all(sent, 'gy', split_axis=0, concat_axis=0, tiled=True)]
    all_to_all x1 -> x0, waiting for transfers between devices: 1.76 us -> none  [shards(): lax.all_to_all(summed, 'gz', split_axis=0, concat_axis=0, tiled=True, axi...]
    pallas_call x9 -> x10, Pallas kernels: 9.74 us -> 8.93 us  [call(): pl.pallas_call(kernel, out_shape=outs, in_specs=[VMEM] * len(args) if spe...]
    ppermute x8, starting transfers between devices: 8.7 us -> 7.92 us  [send(): return lax.ppermute(block, 'gz', along_gz(y, z_lo, core))]
  transfers between devices with their start and end apart: 10 -> 9, of which waited for: 6 -> 6; matrix products, arithmetic and copies ran while one was open for 8% -> 8% of each run, Pallas kernels for 2% -> 4%
where the time goes in v3:
time: 75.7 us; the launch traced here: 75.5 us
  blocking collectives  31.2 us (41%)
  starting transfers between devices  19.4 us (26%)
  waiting for transfers between devices  9.15 us (12%)
  Pallas kernels  8.93 us (12%)
  matrix products  5.82 us (8%)
    all_to_all x1, blocking collectives, shards(): lax.all_to_all(summed, 'gz', split_axis=0, concat_axis=0, tiled=True, axi...  16.3 us
    all_to_all x1, blocking collectives, shards(): cut = lax.all_to_all(cut, 'gy', split_axis=0, concat_axis=0, tiled=True)  15 us
    all_to_all x1, starting transfers between devices, shards(): whole = lax.all_to_all(sent, 'gy', split_axis=0, concat_axis=0, tiled=True)  11.5 us
    pallas_call x10, Pallas kernels, call(): pl.pallas_call(kernel, out_shape=outs, in_specs=[VMEM] * len(args) if spe...  8.93 us
    ppermute x8, starting transfers between devices, send(): return lax.ppermute(block, 'gz', along_gz(y, z_lo, core))  7.92 us
    dot_general x1, matrix products, shards(): one = jnp.dot(flattened.T, flattened, preferred_element_type=F32)  5.82 us
    ppermute x8, waiting for transfers between devices, send(): return lax.ppermute(block, 'gz', along_gz(y, z_lo, core))  5.44 us
    all_to_all x1, waiting for transfers between devices, shards(): whole = lax.all_to_all(sent, 'gy', split_axis=0, concat_axis=0, tiled=True)  3.72 us
  transfers between devices with their start and end apart: 9, of which 6 were waited for; matrix products, arithmetic and copies ran while one was open for 8% of the time, Pallas kernels for 4%

profile of v3, /device:TPU:2, one launch (start us, length us, event | category | flops | bytes accessed | tf_op | source)
XLA Modules:
  0.0 75.5 jit_solution(18127822892426696896)
XLA Ops:
  0.6 4.7 %truncate.1 = bf16[16,208,128]{2,1,0:T(8,128)(2,1)} custom-call(bf16[96,512]{1,0:T(8,128)(2,1)} %bitcast.13, bf16[32,96]{1,0:T(8,128)(2,1)} %b2_ref.1, bf16[4,32,32,512]{3,2,1,0:T(8,128)(2,1)} %field_ref.1), custom_call_target="tpu_custom_call" | custom-call | tf_op jit(solution)/shard_map/truncate/pallas_call | solution.py:25
  5.3 11.5 %all-to-all-start = ((bf16[16,208,128]{2,1,0:T(8,128)(2,1)}), bf16[16,208,128]{2,1,0:T(8,128)(2,1)S(1)}, u32[]{:S(2)}, u32[]{:S(2)}) async-start(bf16[16,208,128]{2,1,0:T(8,128)(2,1)} %truncate.1), calls=%async_computation | async-start | bytes 1703936 | tf_op jit(solution)/shard_map/all_to_all | solution.py:321
  16.8 5.8 %convolution_bitcast_fusion.one_ref = f32[512,512]{1,0:T(8,128)S(1)} fusion(bf16[4,32,32,512]{3,2,1,0:T(8,128)(2,1)} %field_ref.1), kind=kOutput, calls=%fused_computation | convolution fusion | flops 2147483648 | bytes 5242880 | tf_op jit(solution)/shard_map/dot_general | solution.py:324
  22.6 0.6 split.1
  23.4 1.5 %collective-permute-done.1.got_ref = bf16[4,2,128,128]{3,2,1,0:T(8,128)(2,1)S(1)} collective-permute-done((bf16[4,2,128,128]{3,2,1,0:T(8,128)(2,1)S(1)}, bf16[4,2,128,128]{3,2,1,0:T(8,128)(2,1)S(1)}, u32[]{:S(2)}, u32[]{:S(2)}) %collective-permute-start.1) | collective-permute-done | bytes 262176 | tf_op jit(solution)/shard_map/ppermute | solution.py:315
  25.0 1.7 %collective-permute-start.2 = (bf16[2,128,128]{2,1,0:T(8,128)(2,1)S(1)}, bf16[2,128,128]{2,1,0:T(8,128)(2,1)S(1)}, u32[]{:S(2)}, u32[]{:S(2)}) collective-permute-start(bf16[2,128,128]{2,1,0:T(8,128)(2,1)S(1)} %get-tuple-element.25), channel_id=1, source_target_pairs={{0,4},{1,5},{2,6},{3,7},{4,8},{5,9},{6,10},{7,11},{8,12},{9,13},{1... | collective-permute-start | bytes 196616 | tf_op jit(solution)/shard_map/ppermute | solution.py:315
  26.6 2.9 %collective-permute-start.3 = (bf16[2,128,128]{2,1,0:T(8,128)(2,1)S(1)}, bf16[2,128,128]{2,1,0:T(8,128)(2,1)S(1)}, u32[]{:S(2)}, u32[]{:S(2)}) collective-permute-start(bf16[2,128,128]{2,1,0:T(8,128)(2,1)S(1)} %get-tuple-element.26), channel_id=1, source_target_pairs={{0,8},{1,9},{2,10},{3,11},{4,12},{5,13},{6,14},{7,15},{8,0},{9,1},... | collective-permute-start | bytes 196616 | tf_op jit(solution)/shard_map/ppermute | solution.py:315
  29.5 1.3 %collective-permute-start.4 = (bf16[2,128,128]{2,1,0:T(8,128)(2,1)S(1)}, bf16[2,128,128]{2,1,0:T(8,128)(2,1)S(1)}, u32[]{:S(2)}, u32[]{:S(2)}) collective-permute-start(bf16[2,128,128]{2,1,0:T(8,128)(2,1)S(1)} %get-tuple-element.27), channel_id=1, source_target_pairs={{0,12},{1,13},{2,14},{3,15},{4,0},{5,1},{6,2},{7,3},{8,4},{9,5},{1... | collective-permute-start | bytes 196616 | tf_op jit(solution)/shard_map/ppermute | solution.py:315
  30.9 2.2 %collective-permute-done.3.refs_2_ = bf16[2,128,128]{2,1,0:T(8,128)(2,1)S(1)} collective-permute-done((bf16[2,128,128]{2,1,0:T(8,128)(2,1)S(1)}, bf16[2,128,128]{2,1,0:T(8,128)(2,1)S(1)}, u32[]{:S(2)}, u32[]{:S(2)}) %collective-permute-start.3) | collective-permute-done | bytes 65568 | tf_op jit(solution)/shard_map/ppermute | solution.py:315
  33.0 0.8 collective-permute-done.4.refs_3_
  33.8 1.1 %collective-permute-start.5 = (bf16[128,128]{1,0:T(8,128)(2,1)S(1)}, bf16[128,128]{1,0:T(8,128)(2,1)S(1)}, u32[]{:S(2)}, u32[]{:S(2)}) collective-permute-start(bf16[128,128]{1,0:T(8,128)(2,1)S(1)} %get-tuple-element.29), channel_id=1, source_target_pairs={{0,2},{1,3},{2,0},{3,1},{4,6},{5,7},{6,4},{7,5},{8,10},{9,11},{10,... | collective-permute-start | bytes 98312 | tf_op jit(solution)/shard_map/ppermute | solution.py:315
  35.1 3.7 %all-to-all-done.whole_ref = bf16[16,208,128]{2,1,0:T(8,128)(2,1)S(1)} async-done(((bf16[16,208,128]{2,1,0:T(8,128)(2,1)}), bf16[16,208,128]{2,1,0:T(8,128)(2,1)S(1)}, u32[]{:S(2)}, u32[]{:S(2)}) %all-to-all-start) | async-done | bytes 852000 | tf_op jit(solution)/shard_map/all_to_all | solution.py:321
  38.8 0.5 gram_other.1.after_ref
  39.3 0.6 collective-permute-start.6
  39.9 0.1 collective-permute-done.got_ref
  40.1 1.2 %core_part.1 = (bf16[8,112,128]{2,1,0:T(8,128)(2,1)S(1)}, f32[3,768,128]{2,1,0:T(8,128)S(1)}) custom-call(bf16[16,208,128]{2,1,0:T(8,128)(2,1)S(1)} %all-to-all-done.whole_ref, bf16[16,16,128]{2,1,0:T(8,128)(2,1)S(1)} %collective-permute-done.got_ref, bf16[768,256]{1,0:T(8,128)(2,1)S(1)} %select_bitcast_fusion.kron_ref, ...), custom_call_target="tpu_custom_call" | custom-call | tf_op jit(solution)/shard_map/core_part/pallas_call | solution.py:25
  41.2 0.2 collective-permute-start.7
  41.5 0.5 gram_own.1.gram_ref
  41.9 0.9 %collective-permute-done.7.core_got_ref = bf16[8,112,128]{2,1,0:T(8,128)(2,1)S(1)} collective-permute-done((bf16[8,112,128]{2,1,0:T(8,128)(2,1)S(1)}, bf16[8,112,128]{2,1,0:T(8,128)(2,1)S(1)}, u32[]{:S(2)}, u32[]{:S(2)}) %collective-permute-start.7) | collective-permute-done | bytes 229408 | tf_op jit(solution)/shard_map/ppermute | solution.py:315
  42.8 0.3 pair.1
  43.1 16.3 %all_to_all.15.in_ref = bf16[8,240,128]{2,1,0:T(8,128)(2,1)S(1)} all-to-all(bf16[8,240,128]{2,1,0:T(8,128)(2,1)S(1)} %pair.1), channel_id=1, replica_groups={{0,2,4,6,8,10,12,14},{1,3,5,7,9,11,13,15},{16,18,20,22,24,26,28,30},{17..., dimensions={0} | all-to-all | bytes 983040 | tf_op jit(solution)/shard_map/all_to_all | solution.py:343
  59.3 0.3 middle.1
  59.6 15.0 %all_to_all.16.refs_0_ = bf16[16,32,128]{2,1,0:T(8,128)(2,1)S(1)} all-to-all(bf16[16,32,128]{2,1,0:T(8,128)(2,1)S(1)} %middle.1), channel_id=1, replica_groups=mesh['gy'=16,'gz'=16] {'gy'}, dimensions={0} | all-to-all | bytes 262144 | tf_op jit(solution)/shard_map/all_to_all | solution.py:347
  74.6 0.9 %last.1 = (f32[2,512]{1,0:T(2,128)}, f32[2,512]{1,0:T(2,128)}, f32[6,6,4,96]{3,2,1,0:T(4,128)}) custom-call(bf16[16,32,128]{2,1,0:T(8,128)(2,1)S(1)} %all_to_all.16.refs_0_), custom_call_target="tpu_custom_call" | custom-call | tf_op jit(solution)/shard_map/last/pallas_call | solution.py:25
  (15 shorter events, 0.4 us)
Async XLA Ops:
  5.3 33.5 %all-to-all-start = ((bf16[16,208,128]{2,1,0:T(8,128)(2,1)}), bf16[16,208,128]{2,1,0:T(8,128)(2,1)S(1)}, u32[]{:S(2)}, u32[]{:S(2)}) async-start(bf16[16,208,128]{2,1,0:T(8,128)(2,1)} %truncate.1), calls=%async_computation | async-start | bytes 1703936 | tf_op jit(solution)/shard_map/all_to_all | solution.py:321
  16.8 18.1 %copy-start = (bf16[32,96]{1,0:T(8,128)(2,1)S(1)}, bf16[32,96]{1,0:T(8,128)(2,1)}, u32[]{:S(2)}) copy-start(bf16[32,96]{1,0:T(8,128)(2,1)} %param.7) | copy-start | bytes 18436
  23.3 1.6 %collective-permute-start.1 = (bf16[4,2,128,128]{3,2,1,0:T(8,128)(2,1)S(1)}, bf16[4,2,128,128]{3,2,1,0:T(8,128)(2,1)S(1)}, u32[]{:S(2)}, u32[]{:S(2)}) collective-permute-start(bf16[4,2,128,128]{3,2,1,0:T(8,128)(2,1)S(1)} %get-tuple-element.23), channel_id=1, source_target_pairs={{0,1},{1,0},{2,3},{3,2},{4,5},{5,4},{6,7},{7,6},{8,9},{9,8},{10,11... | collective-permute-start | bytes 786440 | tf_op jit(solution)/shard_map/ppermute | solution.py:315
  25.0 5.9 %collective-permute-start.2 = (bf16[2,128,128]{2,1,0:T(8,128)(2,1)S(1)}, bf16[2,128,128]{2,1,0:T(8,128)(2,1)S(1)}, u32[]{:S(2)}, u32[]{:S(2)}) collective-permute-start(bf16[2,128,128]{2,1,0:T(8,128)(2,1)S(1)} %get-tuple-element.25), channel_id=1, source_target_pairs={{0,4},{1,5},{2,6},{3,7},{4,8},{5,9},{6,10},{7,11},{8,12},{9,13},{1... | collective-permute-start | bytes 196616 | tf_op jit(solution)/shard_map/ppermute | solution.py:315
  26.6 6.4 %collective-permute-start.3 = (bf16[2,128,128]{2,1,0:T(8,128)(2,1)S(1)}, bf16[2,128,128]{2,1,0:T(8,128)(2,1)S(1)}, u32[]{:S(2)}, u32[]{:S(2)}) collective-permute-start(bf16[2,128,128]{2,1,0:T(8,128)(2,1)S(1)} %get-tuple-element.26), channel_id=1, source_target_pairs={{0,8},{1,9},{2,10},{3,11},{4,12},{5,13},{6,14},{7,15},{8,0},{9,1},... | collective-permute-start | bytes 196616 | tf_op jit(solution)/shard_map/ppermute | solution.py:315
  29.5 4.3 %collective-permute-start.4 = (bf16[2,128,128]{2,1,0:T(8,128)(2,1)S(1)}, bf16[2,128,128]{2,1,0:T(8,128)(2,1)S(1)}, u32[]{:S(2)}, u32[]{:S(2)}) collective-permute-start(bf16[2,128,128]{2,1,0:T(8,128)(2,1)S(1)} %get-tuple-element.27), channel_id=1, source_target_pairs={{0,12},{1,13},{2,14},{3,15},{4,0},{5,1},{6,2},{7,3},{8,4},{9,5},{1... | collective-permute-start | bytes 196616 | tf_op jit(solution)/shard_map/ppermute | solution.py:315
  33.8 5.0 %collective-permute-start.5 = (bf16[128,128]{1,0:T(8,128)(2,1)S(1)}, bf16[128,128]{1,0:T(8,128)(2,1)S(1)}, u32[]{:S(2)}, u32[]{:S(2)}) collective-permute-start(bf16[128,128]{1,0:T(8,128)(2,1)S(1)} %get-tuple-element.29), channel_id=1, source_target_pairs={{0,2},{1,3},{2,0},{3,1},{4,6},{5,7},{6,4},{7,5},{8,10},{9,11},{10,... | collective-permute-start | bytes 98312 | tf_op jit(solution)/shard_map/ppermute | solution.py:315
  38.8 1.3 %collective-permute-start = (bf16[16,16,128]{2,1,0:T(8,128)(2,1)S(1)}, bf16[16,16,128]{2,1,0:T(8,128)(2,1)S(1)}, u32[]{:S(2)}, u32[]{:S(2)}) collective-permute-start(bf16[16,16,128]{2,1,0:T(8,128)(2,1)S(1)} %slice.4), channel_id=1, source_target_pairs={{0,1},{1,0},{2,3},{3,2},{4,5},{5,4},{6,7},{7,6},{8,9},{9,8},{10,11... | collective-permute-start | bytes 196616 | tf_op jit(solution)/shard_map/ppermute | solution.py:315
  39.3 2.6 %collective-permute-start.6 = (bf16[8,128,128]{2,1,0:T(8,128)(2,1)S(1)}, bf16[8,128,128]{2,1,0:T(8,128)(2,1)S(1)}, u32[]{:S(2)}, u32[]{:S(2)}) collective-permute-start(bf16[8,128,128]{2,1,0:T(8,128)(2,1)S(1)} %gram_other.1.after_ref), channel_id=1, source_target_pairs={{0,1},{1,0},{2,3},{3,2},{4,5},{5,4},{6,7},{7,6},{8,9},{9,8},{10,11... | collective-permute-start | bytes 786440 | tf_op jit(solution)/shard_map/ppermute | solution.py:315
  41.2 1.6 %collective-permute-start.7 = (bf16[8,112,128]{2,1,0:T(8,128)(2,1)S(1)}, bf16[8,112,128]{2,1,0:T(8,128)(2,1)S(1)}, u32[]{:S(2)}, u32[]{:S(2)}) collective-permute-start(bf16[8,112,128]{2,1,0:T(8,128)(2,1)S(1)} %get-tuple-element.30.refs_0_), channel_id=1, source_target_pairs={{0,1},{1,0},{2,3},{3,2},{4,5},{5,4},{6,7},{7,6},{8,9},{9,8},{10,11... | collective-permute-start | bytes 688136 | tf_op jit(solution)/shard_map/ppermute | solution.py:315

commit v4 on v3

--- a/solution.py
+++ b/solution.py
@@ -151,10 +151,7 @@
 along_z = call(along_z_kernel, (shape((128, 128)), shape((128, 128))), name="along_z")
 
 
-def gram_kernel(away, whole_ref, *refs):
-    out_ref, gram = refs[-2:]
-    side = (lax.axis_index("gz") + away) % 2
-
+def gram_rows(whole_ref, side, out_ref, gram):
     def cells(first, size):
         parts = [whole_ref[:, pl.ds(a * 32 + first, size), :] for a in range(6)]
         return jnp.concatenate([part.reshape(16 * size, 128) for part in parts], axis=1)
@@ -168,29 +165,40 @@
             out_ref[b, c * 32 : c * 32 + 32, :] = rows.astype(BF16)
 
 
-def gram_part(away, whole, *after):
-    return call(
-        functools.partial(gram_kernel, away),
-        shape((8, 128, 128)),
-        [pltpu.VMEM((1024, 128), F32)],
-        [VMEM] + [ANY] * len(after),
-        name="gram_other" if away else "gram_own",
-    )(whole, *after)
-
-
-def core_rows(parts_ref, b, side):
-    pieces = []
-    for t in range(6):
-        at = pl.multiple_of((side + b * 2) * 48 + t * 8, 8)
-        pieces += [parts_ref[a, pl.ds(at, 8), :] for a in range(3)]
-    rest = jnp.concatenate(pieces[14:], axis=0)
-    rest = [pltpu.roll(rest, 96 - 32 * g, 1) for g in range(3)]
-    rest = jnp.concatenate(rest + [jnp.zeros((16, 128), F32)], axis=0)
+def core_rows(kron_ref, high_ref, low_ref, side, out_ref):
+    kron = kron_ref[pl.ds(pl.multiple_of(side * 384, 384), 384), :]
+    parts = []
+    for a in range(3):
+        lanes = slice(a * 256, (a + 1) * 256)
+        parts.append(nt_dot(kron, high_ref[:, lanes]) + nt_dot(kron, low_ref[:, lanes]))
     lane = lax.broadcasted_iota(jnp.int32, (112, 128), 1)
-    return jnp.where(lane < 96, jnp.concatenate(pieces[:14], axis=0), rest)
-
-
-def core_kernel(whole_ref, got_ref, kron_ref, after_ref, other_ref, parts_ref, basis):
+    for b in range(8):
+        pieces = []
+        for t in range(6):
+            at = b * 48 + t * 8
+            pieces += [part[at : at + 8] for part in parts]
+        rest = jnp.concatenate(pieces[14:], axis=0)
+        rest = [pltpu.roll(rest, 96 - 32 * g, 1) for g in range(3)]
+        rest = jnp.concatenate(rest + [jnp.zeros((16, 128), F32)], axis=0)
+        packed = jnp.where(lane < 96, jnp.concatenate(pieces[:14], axis=0), rest)
+        out_ref[b] = packed.astype(out_ref.dtype)
+
+
+def gram_kernel(whole_ref, after_ref, out_ref, gram):
+    gram_rows(whole_ref, 1 - lax.axis_index("gz") % 2, out_ref, gram)
+
+
+gram_part = call(
+    gram_kernel,
+    shape((8, 128, 128)),
+    [pltpu.VMEM((1024, 128), F32)],
+    [VMEM, ANY],
+    name="gram_other",
+)
+
+
+def core_kernel(whole_ref, got_ref, kron_ref, *refs):
+    out_ref, high_ref, low_ref, basis = refs[-4:]
     core = lax.axis_index("gz") % 2
     basis[:, core] = whole_ref[:, 192:208, :]
     basis[:, 1 - core] = got_ref[...]
@@ -201,30 +209,38 @@
         (((0,), (0,)), ((), ())),
         preferred_element_type=F32,
     )
-    high = mixed.astype(BF16)
-    low = (mixed - high.astype(F32)).astype(BF16)
-    for a in range(3):
-        lanes = slice(a * 256, (a + 1) * 256)
-        parts_ref[a] = nt_dot(kron_ref[...], high[:, lanes]) + nt_dot(kron_ref[...], low[:, lanes])
-    for b in range(8):
-        other_ref[b] = core_rows(parts_ref, b, 1 - core).astype(BF16)
+    high_ref[...] = mixed.astype(BF16)
+    low_ref[...] = (mixed - high_ref[...].astype(F32)).astype(BF16)
+    core_rows(kron_ref, high_ref, low_ref, 1 - core, out_ref)
 
 
 core_part = call(
     core_kernel,
-    (shape((8, 112, 128)), shape((3, 768, 128), F32)),
+    (shape((8, 112, 128)), shape((128, 768)), shape((128, 768))),
     [pltpu.VMEM((16, 2, 16, 128), BF16)],
-    [VMEM, VMEM, VMEM, ANY],
-    name="core_part",
-)
-
-
-def pair_kernel(gram_ref, gram_got_ref, parts_ref, core_got_ref, out_ref):
+    [VMEM, VMEM, VMEM, ANY, ANY],
+    name="core_other",
+)
+
+
+def own_kernel(whole_ref, kron_ref, high_ref, low_ref, after_ref, gram_ref, core_ref, gram):
     core = lax.axis_index("gz") % 2
+    gram_rows(whole_ref, core, gram_ref, gram)
+    core_rows(kron_ref, high_ref, low_ref, core, core_ref)
+
+
+own_part = call(
+    own_kernel,
+    (shape((8, 128, 128)), shape((8, 112, 128), F32)),
+    [pltpu.VMEM((1024, 128), F32)],
+    [VMEM] * 4 + [ANY],
+    name="own",
+)
+
+
+def pair_kernel(gram_ref, gram_got_ref, core_ref, core_got_ref, out_ref):
     out_ref[:, 0:128, :] = (gram_ref[...].astype(F32) + gram_got_ref[...].astype(F32)).astype(BF16)
-    for b in range(8):
-        total = core_rows(parts_ref, b, core) + core_got_ref[b].astype(F32)
-        out_ref[b, 128:240, :] = total.astype(BF16)
+    out_ref[:, 128:240, :] = (core_ref[...] + core_got_ref[...].astype(F32)).astype(BF16)
 
 
 pair = call(pair_kernel, shape((8, 240, 128)), name="pair")
@@ -240,32 +256,37 @@
     for c in range(4):
         for e in range(2):
             at = c * 32 + e * 16
-            cut[pl.ds(e * 4 + c, 16, stride=32), :] = one[at : at + 16]
-            cut[pl.ds(8 + e * 4 + c, 16, stride=32), :] = sums[pl.ds(c * 32 + e, 16, stride=2), :]
+            cut[pl.ds(e * 4 + c, 16, stride=24), :] = one[at : at + 16]
+            cut[pl.ds(8 + e * 4 + c, 16, stride=24), :] = sums[pl.ds(c * 32 + e, 16, stride=2), :]
     rest = [pltpu.roll(total[128 + g * 32 : 160 + g * 32], (32 + 32 * g) % 128, 1) for g in range(3)]
     lane = lax.broadcasted_iota(jnp.int32, (32, 128), 1)
     rest = jnp.where(lane < 32, rest[0], jnp.where(lane < 64, rest[1], rest[2]))
     core[0:128, :] = jnp.concatenate([total[128:240], rest[0:16]], axis=0).T
     tail = jnp.concatenate([rest[16:32], jnp.zeros((112, 128), F32)], axis=0)
     core[128:256, :] = tail.T
+    lane = lax.broadcasted_iota(jnp.int32, (16, 128), 1) // 16
+    last = jnp.zeros((16, 128), F32)
     for s in range(6):
-        cut[pl.ds(16 + s, 16, stride=32), :] = core[pl.ds(s, 16, stride=6), :]
-        cut[pl.ds(22 + s, 16, stride=32), :] = core[pl.ds(128 + s, 16, stride=6), :]
-    out_ref[...] = cut[...].astype(BF16).reshape(16, 32, 128)
+        cut[pl.ds(16 + s, 16, stride=24), :] = core[pl.ds(s, 16, stride=6), :]
+        part = core[pl.ds(128 + s, 16, stride=6), :]
+        last = jnp.where(lane == s, pltpu.roll(part, 16 * s, 1) if s else part, last)
+    cut[pl.ds(22, 16, stride=24), :] = last
+    out_ref[...] = cut[...].reshape(16, 24, 128).astype(BF16)
 
 
 middle = call(
     middle_kernel,
-    shape((16, 32, 128)),
-    [pltpu.VMEM((128, 128), F32), pltpu.VMEM((256, 128), F32), pltpu.VMEM((512, 128), F32)],
+    shape((16, 24, 128)),
+    [pltpu.VMEM((128, 128), F32), pltpu.VMEM((256, 128), F32), pltpu.VMEM((384, 128), F32)],
     name="middle",
 )
 
 
 def last_kernel(scale_one, scale_two, in_ref, one_ref, two_ref, core_ref, turned, ordered, core):
-    total = in_ref[0, 0:16, :].astype(F32)
+    got = in_ref[...].astype(F32)
+    total = got[0, 0:16]
     for source in range(1, 16):
-        total = total + in_ref[source, 0:16, :].astype(F32)
+        total = total + got[source, 0:16]
     turned[...] = jnp.concatenate([total[8:16], jnp.zeros((120, 128), F32)], axis=0).T
     for group in range(4):
         for jj in range(4):
@@ -277,20 +298,23 @@
             lanes = slice(c * 128, (c + 1) * 128)
             one_ref[e : e + 1, lanes] = total[e * 4 + c : e * 4 + c + 1] * scale_one
             two_ref[e : e + 1, lanes] = two[e * 4 + c : e * 4 + c + 1] * scale_two
-    lane = lax.broadcasted_iota(jnp.int32, (16, 128), 1)
+    lane = lax.broadcasted_iota(jnp.int32, (8, 128), 1)
+    row = lax.broadcasted_iota(jnp.int32, (8, 128), 0)
     for v in range(4):
-        blocks = [in_ref[v * 4 + g, 16:32, :].astype(F32) for g in range(4)]
+        blocks = [got[v * 4 + g, 16:24] for g in range(4)]
         for t in range(6):
-            row = jnp.zeros((16, 128), F32)
+            ranks = jnp.zeros((8, 128), F32)
             for g in range(4):
                 shift = (24 * (g - t)) % 128
                 moved = pltpu.roll(blocks[g], shift, 1) if shift else blocks[g]
                 if t == 5:
-                    rest = jnp.concatenate([blocks[g][6:16], blocks[g][0:6]], axis=0)
-                    rest = pltpu.roll(rest, 24 * g + 8, 1)
+                    rest = jnp.zeros((8, 128), F32)
+                    for s in range(6):
+                        turned = pltpu.roll(blocks[g], (24 * g + 8 - 16 * s) % 128, 1)
+                        rest = jnp.where(row == s, turned[6:7], rest)
                     moved = jnp.where(lane < 24 * g + 8, moved, rest)
-                row = jnp.where((lane >= 24 * g) & (lane < 24 * g + 24), moved, row)
-            core[pl.ds(t * 4 + v, 8, stride=24), :] = row[0:8]
+                ranks = jnp.where((lane >= 24 * g) & (lane < 24 * g + 24), moved, ranks)
+            core[pl.ds(t * 4 + v, 8, stride=24), :] = ranks
     for s in range(6):
         for t in range(6):
             core_ref[s, t] = core[(s * 6 + t) * 4 : (s * 6 + t) * 4 + 4, 0:96]
@@ -328,17 +352,18 @@
     other, one_own = along_z(*blocks)
     one_got = send(other, z_lo=1)
 
-    repeated = jnp.tile(basis_three.T, (1, 8))[:, None, :]
+    turned = jnp.transpose(basis_three.reshape(32, 8, 2, 6), (2, 1, 3, 0)).reshape(96, 32)
+    repeated = jnp.tile(turned, (1, 8))[:, None, :]
     same = jnp.arange(8)[:, None] == jnp.arange(256)[None, :] // 32
     kron = jnp.where(same[None], repeated, jnp.zeros((), BF16)).reshape(768, 256)
 
     basis_got = send(whole[:, 192:208], core=1)
-    gram_other = gram_part(1, whole, one_own, one_got)
+    gram_other = gram_part(whole, one_own)
     gram_got = send(gram_other, core=1)
-    core_other, core_parts = core_part(whole, basis_got, kron, gram_other)
+    core_other, high, low = core_part(whole, basis_got, kron, gram_other, one_got)
     core_got = send(core_other, core=1)
-    gram_own = gram_part(0, whole, core_other)
-    summed = pair(gram_own, gram_got, core_parts, core_got)
+    gram_own, core_own = own_part(whole, kron, high, low, core_other)
+    summed = pair(gram_own, gram_got, core_own, core_got)
     groups = [[2 * b + core for b in range(8)] for core in range(2)]
     summed = lax.all_to_all(
         summed, "gz", split_axis=0, concat_axis=0, tiled=True, axis_index_groups=groups

time: 75.7 us -> 74.7 us (0.987)
    ppermute x8, waiting for transfers between devices: 5.44 us -> 4.64 us  [send(): return lax.ppermute(block, 'gz', along_gz(y, z_lo, core))]
where the time goes in v4:
time: 74.7 us; the launch traced here: 74.4 us
  blocking collectives  30.6 us (41%)
  starting transfers between devices  19.4 us (26%)
  Pallas kernels  8.89 us (12%)
  waiting for transfers between devices  8.49 us (11%)
  matrix products  5.82 us (8%)
  between operations  0.78 us (1%)
    all_to_all x1, blocking collectives, shards(): lax.all_to_all(summed, 'gz', split_axis=0, concat_axis=0, tiled=True, axi...  16.3 us
    all_to_all x1, blocking collectives, shards(): cut = lax.all_to_all(cut, 'gy', split_axis=0, concat_axis=0, tiled=True)  14.4 us
    all_to_all x1, starting transfers between devices, shards(): whole = lax.all_to_all(sent, 'gy', split_axis=0, concat_axis=0, tiled=True)  11.5 us
    pallas_call x10, Pallas kernels, call(): pl.pallas_call(kernel, out_shape=outs, in_specs=[VMEM] * len(args) if spe...  8.89 us
    ppermute x8, starting transfers between devices, send(): return lax.ppermute(block, 'gz', along_gz(y, z_lo, core))  7.92 us
    dot_general x1, matrix products, shards(): one = jnp.dot(flattened.T, flattened, preferred_element_type=F32)  5.82 us
    ppermute x8, waiting for transfers between devices, send(): return lax.ppermute(block, 'gz', along_gz(y, z_lo, core))  4.64 us
    all_to_all x1, waiting for transfers between devices, shards(): whole = lax.all_to_all(sent, 'gy', split_axis=0, concat_axis=0, tiled=True)  3.85 us
  transfers between devices with their start and end apart: 9, of which 6 were waited for; matrix products, arithmetic and copies ran while one was open for 8% of the time, Pallas kernels for 4%

profile of v4, /device:TPU:2, one launch (start us, length us, event | category | flops | bytes accessed | tf_op | source)
XLA Modules:
  0.0 74.4 jit_solution(6357380388412958551)
XLA Ops:
  0.6 4.7 %truncate.1 = bf16[16,208,128]{2,1,0:T(8,128)(2,1)} custom-call(bf16[96,512]{1,0:T(8,128)(2,1)} %bitcast.16, bf16[32,96]{1,0:T(8,128)(2,1)} %b2_ref.1, bf16[4,32,32,512]{3,2,1,0:T(8,128)(2,1)} %field_ref.1), custom_call_target="tpu_custom_call" | custom-call | tf_op jit(solution)/shard_map/truncate/pallas_call | solution.py:25
  5.3 11.5 %all-to-all-start = ((bf16[16,208,128]{2,1,0:T(8,128)(2,1)}), bf16[16,208,128]{2,1,0:T(8,128)(2,1)S(1)}, u32[]{:S(2)}, u32[]{:S(2)}) async-start(bf16[16,208,128]{2,1,0:T(8,128)(2,1)} %truncate.1), calls=%async_computation | async-start | bytes 1703936 | tf_op jit(solution)/shard_map/all_to_all | solution.py:345
  16.8 5.8 %convolution_bitcast_fusion.one_ref = f32[512,512]{1,0:T(8,128)S(1)} fusion(bf16[4,32,32,512]{3,2,1,0:T(8,128)(2,1)} %field_ref.1), kind=kOutput, calls=%fused_computation | convolution fusion | flops 2147483648 | bytes 5242880 | tf_op jit(solution)/shard_map/dot_general | solution.py:348
  22.6 0.6 split.1
  23.4 1.5 %collective-permute-done.1.got_ref = bf16[4,2,128,128]{3,2,1,0:T(8,128)(2,1)S(1)} collective-permute-done((bf16[4,2,128,128]{3,2,1,0:T(8,128)(2,1)S(1)}, bf16[4,2,128,128]{3,2,1,0:T(8,128)(2,1)S(1)}, u32[]{:S(2)}, u32[]{:S(2)}) %collective-permute-start.1) | collective-permute-done | bytes 262176 | tf_op jit(solution)/shard_map/ppermute | solution.py:339
  25.0 1.7 %collective-permute-start.2 = (bf16[2,128,128]{2,1,0:T(8,128)(2,1)S(1)}, bf16[2,128,128]{2,1,0:T(8,128)(2,1)S(1)}, u32[]{:S(2)}, u32[]{:S(2)}) collective-permute-start(bf16[2,128,128]{2,1,0:T(8,128)(2,1)S(1)} %get-tuple-element.28), channel_id=1, source_target_pairs={{0,4},{1,5},{2,6},{3,7},{4,8},{5,9},{6,10},{7,11},{8,12},{9,13},{1... | collective-permute-start | bytes 196616 | tf_op jit(solution)/shard_map/ppermute | solution.py:339
  26.6 2.9 %collective-permute-start.3 = (bf16[2,128,128]{2,1,0:T(8,128)(2,1)S(1)}, bf16[2,128,128]{2,1,0:T(8,128)(2,1)S(1)}, u32[]{:S(2)}, u32[]{:S(2)}) collective-permute-start(bf16[2,128,128]{2,1,0:T(8,128)(2,1)S(1)} %get-tuple-element.29), channel_id=1, source_target_pairs={{0,8},{1,9},{2,10},{3,11},{4,12},{5,13},{6,14},{7,15},{8,0},{9,1},... | collective-permute-start | bytes 196616 | tf_op jit(solution)/shard_map/ppermute | solution.py:339
  29.5 1.3 %collective-permute-start.4 = (bf16[2,128,128]{2,1,0:T(8,128)(2,1)S(1)}, bf16[2,128,128]{2,1,0:T(8,128)(2,1)S(1)}, u32[]{:S(2)}, u32[]{:S(2)}) collective-permute-start(bf16[2,128,128]{2,1,0:T(8,128)(2,1)S(1)} %get-tuple-element.30), channel_id=1, source_target_pairs={{0,12},{1,13},{2,14},{3,15},{4,0},{5,1},{6,2},{7,3},{8,4},{9,5},{1... | collective-permute-start | bytes 196616 | tf_op jit(solution)/shard_map/ppermute | solution.py:339
  30.9 0.1 copy.7
  31.3 1.8 %collective-permute-done.3.refs_2_ = bf16[2,128,128]{2,1,0:T(8,128)(2,1)S(1)} collective-permute-done((bf16[2,128,128]{2,1,0:T(8,128)(2,1)S(1)}, bf16[2,128,128]{2,1,0:T(8,128)(2,1)S(1)}, u32[]{:S(2)}, u32[]{:S(2)}) %collective-permute-start.3) | collective-permute-done | bytes 65568 | tf_op jit(solution)/shard_map/ppermute | solution.py:339
  33.0 0.8 %collective-permute-done.4.refs_3_ = bf16[2,128,128]{2,1,0:T(8,128)(2,1)S(1)} collective-permute-done((bf16[2,128,128]{2,1,0:T(8,128)(2,1)S(1)}, bf16[2,128,128]{2,1,0:T(8,128)(2,1)S(1)}, u32[]{:S(2)}, u32[]{:S(2)}) %collective-permute-start.4) | collective-permute-done | bytes 65568 | tf_op jit(solution)/shard_map/ppermute | solution.py:339
  33.8 1.1 %collective-permute-start.5 = (bf16[128,128]{1,0:T(8,128)(2,1)S(1)}, bf16[128,128]{1,0:T(8,128)(2,1)S(1)}, u32[]{:S(2)}, u32[]{:S(2)}) collective-permute-start(bf16[128,128]{1,0:T(8,128)(2,1)S(1)} %get-tuple-element.32), channel_id=1, source_target_pairs={{0,2},{1,3},{2,0},{3,1},{4,6},{5,7},{6,4},{7,5},{8,10},{9,11},{10,... | collective-permute-start | bytes 98312 | tf_op jit(solution)/shard_map/ppermute | solution.py:339
  35.0 3.8 %all-to-all-done.whole_ref = bf16[16,208,128]{2,1,0:T(8,128)(2,1)S(1)} async-done(((bf16[16,208,128]{2,1,0:T(8,128)(2,1)}), bf16[16,208,128]{2,1,0:T(8,128)(2,1)S(1)}, u32[]{:S(2)}, u32[]{:S(2)}) %all-to-all-start) | async-done | bytes 852000 | tf_op jit(solution)/shard_map/all_to_all | solution.py:345
  38.8 0.5 gram_other.1.refs_0_
  39.3 0.6 collective-permute-start.6
  39.9 0.1 collective-permute-done.got_ref
  40.1 0.8 %core_other.1 = (bf16[8,112,128]{2,1,0:T(8,128)(2,1)S(1)}, bf16[128,768]{1,0:T(8,128)(2,1)S(1)}, bf16[128,768]{1,0:T(8,128)(2,1)S(1)}) custom-call(bf16[16,208,128]{2,1,0:T(8,128)(2,1)S(1)} %all-to-all-done.whole_ref, bf16[16,16,128]{2,1,0:T(8,128)(2,1)S(1)} %collective-permute-done.got_ref, bf16[768,256]{1,0:T(8,128)(2,1)S(1)} %select_bitcast_fusion.kron_ref, ...), custom_call_target="tpu_custom_call" | custom-call | tf_op jit(solution)/shard_map/core_other/pallas_call | solution.py:25
  40.9 0.2 collective-permute-start.7
  41.1 0.8 %own.1 = (bf16[8,128,128]{2,1,0:T(8,128)(2,1)S(1)}, f32[8,112,128]{2,1,0:T(8,128)S(1)}) custom-call(bf16[16,208,128]{2,1,0:T(8,128)(2,1)S(1)} %all-to-all-done.whole_ref, bf16[768,256]{1,0:T(8,128)(2,1)S(1)} %select_bitcast_fusion.kron_ref, bf16[128,768]{1,0:T(8,128)(2,1)S(1)} %get-tuple-element.33.high_ref, bf16[128,768]{1,0:T(8,128)(2,1)S(1)} %get-tuple-element.34.low_ref, ...), custom_call_target="tpu_custom_call" | custom-call | tf_op jit(solution)/shard_map/own/pallas_call | solution.py:25
  42.0 0.5 collective-permute-done.7.core_got_ref
  42.6 16.3 %all_to_all.15.in_ref = bf16[8,240,128]{2,1,0:T(8,128)(2,1)S(1)} all-to-all(bf16[8,240,128]{2,1,0:T(8,128)(2,1)S(1)} %pair.1), channel_id=1, replica_groups={{0,2,4,6,8,10,12,14},{1,3,5,7,9,11,13,15},{16,18,20,22,24,26,28,30},{17..., dimensions={0} | all-to-all | bytes 983040 | tf_op jit(solution)/shard_map/all_to_all | solution.py:368
  58.8 0.3 middle.1
  59.2 14.4 %all_to_all.16.refs_0_ = bf16[16,24,128]{2,1,0:T(8,128)(2,1)S(1)} all-to-all(bf16[16,24,128]{2,1,0:T(8,128)(2,1)S(1)} %middle.1), channel_id=1, replica_groups=mesh['gy'=16,'gz'=16] {'gy'}, dimensions={0} | all-to-all | bytes 196608 | tf_op jit(solution)/shard_map/all_to_all | solution.py:372
  73.5 0.9 %last.1 = (f32[2,512]{1,0:T(2,128)}, f32[2,512]{1,0:T(2,128)}, f32[6,6,4,96]{3,2,1,0:T(4,128)}) custom-call(bf16[16,24,128]{2,1,0:T(8,128)(2,1)S(1)} %all_to_all.16.refs_0_), custom_call_target="tpu_custom_call" | custom-call | tf_op jit(solution)/shard_map/last/pallas_call | solution.py:25
  (20 shorter events, 0.6 us)
Async XLA Ops:
  5.3 33.5 %all-to-all-start = ((bf16[16,208,128]{2,1,0:T(8,128)(2,1)}), bf16[16,208,128]{2,1,0:T(8,128)(2,1)S(1)}, u32[]{:S(2)}, u32[]{:S(2)}) async-start(bf16[16,208,128]{2,1,0:T(8,128)(2,1)} %truncate.1), calls=%async_computation | async-start | bytes 1703936 | tf_op jit(solution)/shard_map/all_to_all | solution.py:345
  16.8 14.1 %copy-start = (bf16[32,96]{1,0:T(8,128)(2,1)S(1)}, bf16[32,96]{1,0:T(8,128)(2,1)}, u32[]{:S(2)}) copy-start(bf16[32,96]{1,0:T(8,128)(2,1)} %param.7) | copy-start | bytes 18436
  23.3 1.6 %collective-permute-start.1 = (bf16[4,2,128,128]{3,2,1,0:T(8,128)(2,1)S(1)}, bf16[4,2,128,128]{3,2,1,0:T(8,128)(2,1)S(1)}, u32[]{:S(2)}, u32[]{:S(2)}) collective-permute-start(bf16[4,2,128,128]{3,2,1,0:T(8,128)(2,1)S(1)} %get-tuple-element.26), channel_id=1, source_target_pairs={{0,1},{1,0},{2,3},{3,2},{4,5},{5,4},{6,7},{7,6},{8,9},{9,8},{10,11... | collective-permute-start | bytes 786440 | tf_op jit(solution)/shard_map/ppermute | solution.py:339
  25.0 6.3 %collective-permute-start.2 = (bf16[2,128,128]{2,1,0:T(8,128)(2,1)S(1)}, bf16[2,128,128]{2,1,0:T(8,128)(2,1)S(1)}, u32[]{:S(2)}, u32[]{:S(2)}) collective-permute-start(bf16[2,128,128]{2,1,0:T(8,128)(2,1)S(1)} %get-tuple-element.28), channel_id=1, source_target_pairs={{0,4},{1,5},{2,6},{3,7},{4,8},{5,9},{6,10},{7,11},{8,12},{9,13},{1... | collective-permute-start | bytes 196616 | tf_op jit(solution)/shard_map/ppermute | solution.py:339
  26.6 6.4 %collective-permute-start.3 = (bf16[2,128,128]{2,1,0:T(8,128)(2,1)S(1)}, bf16[2,128,128]{2,1,0:T(8,128)(2,1)S(1)}, u32[]{:S(2)}, u32[]{:S(2)}) collective-permute-start(bf16[2,128,128]{2,1,0:T(8,128)(2,1)S(1)} %get-tuple-element.29), channel_id=1, source_target_pairs={{0,8},{1,9},{2,10},{3,11},{4,12},{5,13},{6,14},{7,15},{8,0},{9,1},... | collective-permute-start | bytes 196616 | tf_op jit(solution)/shard_map/ppermute | solution.py:339
  29.5 4.3 %collective-permute-start.4 = (bf16[2,128,128]{2,1,0:T(8,128)(2,1)S(1)}, bf16[2,128,128]{2,1,0:T(8,128)(2,1)S(1)}, u32[]{:S(2)}, u32[]{:S(2)}) collective-permute-start(bf16[2,128,128]{2,1,0:T(8,128)(2,1)S(1)} %get-tuple-element.30), channel_id=1, source_target_pairs={{0,12},{1,13},{2,14},{3,15},{4,0},{5,1},{6,2},{7,3},{8,4},{9,5},{1... | collective-permute-start | bytes 196616 | tf_op jit(solution)/shard_map/ppermute | solution.py:339
  33.8 6.1 %collective-permute-start.5 = (bf16[128,128]{1,0:T(8,128)(2,1)S(1)}, bf16[128,128]{1,0:T(8,128)(2,1)S(1)}, u32[]{:S(2)}, u32[]{:S(2)}) collective-permute-start(bf16[128,128]{1,0:T(8,128)(2,1)S(1)} %get-tuple-element.32), channel_id=1, source_target_pairs={{0,2},{1,3},{2,0},{3,1},{4,6},{5,7},{6,4},{7,5},{8,10},{9,11},{10,... | collective-permute-start | bytes 98312 | tf_op jit(solution)/shard_map/ppermute | solution.py:339
  38.8 1.3 %collective-permute-start = (bf16[16,16,128]{2,1,0:T(8,128)(2,1)S(1)}, bf16[16,16,128]{2,1,0:T(8,128)(2,1)S(1)}, u32[]{:S(2)}, u32[]{:S(2)}) collective-permute-start(bf16[16,16,128]{2,1,0:T(8,128)(2,1)S(1)} %slice.4), channel_id=1, source_target_pairs={{0,1},{1,0},{2,3},{3,2},{4,5},{5,4},{6,7},{7,6},{8,9},{9,8},{10,11... | collective-permute-start | bytes 196616 | tf_op jit(solution)/shard_map/ppermute | solution.py:339
  39.3 2.7 %collective-permute-start.6 = (bf16[8,128,128]{2,1,0:T(8,128)(2,1)S(1)}, bf16[8,128,128]{2,1,0:T(8,128)(2,1)S(1)}, u32[]{:S(2)}, u32[]{:S(2)}) collective-permute-start(bf16[8,128,128]{2,1,0:T(8,128)(2,1)S(1)} %gram_other.1.refs_0_), channel_id=1, source_target_pairs={{0,1},{1,0},{2,3},{3,2},{4,5},{5,4},{6,7},{7,6},{8,9},{9,8},{10,11... | collective-permute-start | bytes 786440 | tf_op jit(solution)/shard_map/ppermute | solution.py:339
  40.9 1.6 %collective-permute-start.7 = (bf16[8,112,128]{2,1,0:T(8,128)(2,1)S(1)}, bf16[8,112,128]{2,1,0:T(8,128)(2,1)S(1)}, u32[]{:S(2)}, u32[]{:S(2)}) collective-permute-start(bf16[8,112,128]{2,1,0:T(8,128)(2,1)S(1)} %get-tuple-element.35.after_ref), channel_id=1, source_target_pairs={{0,1},{1,0},{2,3},{3,2},{4,5},{5,4},{6,7},{7,6},{8,9},{9,8},{10,11... | collective-permute-start | bytes 688136 | tf_op jit(solution)/shard_map/ppermute | solution.py:339

commit v5 on v4

--- a/solution.py
+++ b/solution.py
@@ -37,21 +37,16 @@
     return jax.ShapeDtypeStruct(dims, dtype)
 
 
-def truncate_kernel(b1t_ref, b2_ref, field_ref, out_ref, b1t, b2, b2_wide, cells, rows, tiles, sent, sems):
+def truncate_kernel(b1t_ref, b2_ref, field_ref, out_ref, *scratch):
+    b1t, b2, b2_wide, cells, *work, sent, sems = scratch
     core = lax.axis_index("gz") % 2
     small = [
         pltpu.make_async_copy(b1t_ref, b1t, sems.at[0]),
         pltpu.make_async_copy(b2_ref, b2, sems.at[1]),
     ]
-    for copy in small:
+    copies = [pltpu.make_async_copy(field_ref.at[v], cells.at[v], sems.at[2 + v]) for v in range(4)]
+    for copy in small + copies:
         copy.start()
-    copies = []
-    for piece in range(8):
-        v, half = piece // 2, pl.ds(piece % 2 * 16, 16)
-        copies.append(
-            pltpu.make_async_copy(field_ref.at[v, half], cells.at[v, half], sems.at[2 + piece])
-        )
-        copies[-1].start()
     for copy in small:
         copy.wait()
     b2_wide[...] = jnp.zeros_like(b2_wide)
@@ -61,13 +56,15 @@
     for peer in range(16):
         sent[peer, 192:208, :] = share
     lane = lax.broadcasted_iota(jnp.int32, (8, 128), 1) // 32
-    outs = []
-    for v in range(4):
-        for copy in copies[v * 2 : v * 2 + 2]:
-            copy.wait()
+
+    def product(v):
+        rows = work[v % 2]
         trunc = nt_dot(b1t[...], cells[v].reshape(1024, 512))
         for b in range(8):
             rows[pl.ds(b, 96, stride=8), :] = trunc[:, b * 128 : (b + 1) * 128]
+
+    def arrange(v):
+        rows, tiles = work[v % 2], work[2 + v % 2]
         for block in range(24):
             first = block * 32
             part = [rows[first + rr * 8 : first + rr * 8 + 8, :] for rr in range(4)]
@@ -79,10 +76,18 @@
                 low = jnp.where(lane == 0, moved[0], moved[1])
                 high = jnp.where(lane == 2, moved[2], moved[3])
                 tiles[first + jj * 8 : first + jj * 8 + 8, :] = jnp.where(lane < 2, low, high)
-        block = slice(v * 4, v * 4 + 4)
-        sent[block, 0:192, :] = tiles[...].astype(BF16).reshape(4, 192, 128)
-        outs.append(pltpu.make_async_copy(sent.at[block], out_ref.at[block], sems.at[10 + v]))
-        outs[-1].start()
+        sent[v * 4 : v * 4 + 4, 0:192, :] = tiles[...].astype(BF16).reshape(4, 192, 128)
+
+    outs = []
+    for v in range(5):
+        if v < 4:
+            copies[v].wait()
+            product(v)
+        if v > 0:
+            arrange(v - 1)
+            block = slice(v * 4 - 4, v * 4)
+            outs.append(pltpu.make_async_copy(sent.at[block], out_ref.at[block], sems.at[5 + v]))
+            outs[-1].start()
     for copy in outs:
         copy.wait()
 
@@ -95,10 +100,9 @@
         pltpu.VMEM((32, 96), BF16),
         pltpu.VMEM((32, 128), F32),
         pltpu.VMEM((4, 32, 32, 512), BF16),
-        pltpu.VMEM((768, 128), F32),
-        pltpu.VMEM((768, 128), F32),
+        *[pltpu.VMEM((768, 128), F32)] * 4,
         pltpu.VMEM((16, 208, 128), BF16),
-        pltpu.SemaphoreType.DMA((14,)),
+        pltpu.SemaphoreType.DMA((10,)),
     ],
     [HBM, HBM, HBM],
     WIDE,

time: 74.7 us -> 74.1 us (level)
  no operation moved by 1% of the time
where the time goes in v5:
time: 74.1 us; the launch traced here: 73.8 us
  blocking collectives  30.6 us (41%)
  starting transfers between devices  19.4 us (26%)
  waiting for transfers between devices  8.48 us (11%)
  Pallas kernels  8.3 us (11%)
  matrix products  5.82 us (8%)
  between operations  0.78 us (1%)
    all_to_all x1, blocking collectives, shards(): lax.all_to_all(summed, 'gz', split_axis=0, concat_axis=0, tiled=True, axi...  16.2 us
    all_to_all x1, blocking collectives, shards(): cut = lax.all_to_all(cut, 'gy', split_axis=0, concat_axis=0, tiled=True)  14.4 us
    all_to_all x1, starting transfers between devices, shards(): whole = lax.all_to_all(sent, 'gy', split_axis=0, concat_axis=0, tiled=True)  11.5 us
    pallas_call x10, Pallas kernels, call(): pl.pallas_call(kernel, out_shape=outs, in_specs=[VMEM] * len(args) if spe...  8.3 us
    ppermute x8, starting transfers between devices, send(): return lax.ppermute(block, 'gz', along_gz(y, z_lo, core))  7.93 us
    dot_general x1, matrix products, shards(): one = jnp.dot(flattened.T, flattened, preferred_element_type=F32)  5.82 us
    ppermute x8, waiting for transfers between devices, send(): return lax.ppermute(block, 'gz', along_gz(y, z_lo, core))  4.62 us
    all_to_all x1, waiting for transfers between devices, shards(): whole = lax.all_to_all(sent, 'gy', split_axis=0, concat_axis=0, tiled=True)  3.85 us
  transfers between devices with their start and end apart: 9, of which 6 were waited for; matrix products, arithmetic and copies ran while one was open for 8% of the time, Pallas kernels for 4%

profile of v5, /device:TPU:2, one launch (start us, length us, event | category | flops | bytes accessed | tf_op | source)
XLA Modules:
  0.0 73.8 jit_solution(6764661621648883393)
XLA Ops:
  0.6 4.1 %truncate.1 = bf16[16,208,128]{2,1,0:T(8,128)(2,1)} custom-call(bf16[96,512]{1,0:T(8,128)(2,1)} %bitcast.16, bf16[32,96]{1,0:T(8,128)(2,1)} %b2_ref.1, bf16[4,32,32,512]{3,2,1,0:T(8,128)(2,1)} %field_ref.1), custom_call_target="tpu_custom_call" | custom-call | tf_op jit(solution)/shard_map/truncate/pallas_call | solution.py:25
  4.7 11.5 %all-to-all-start = ((bf16[16,208,128]{2,1,0:T(8,128)(2,1)}), bf16[16,208,128]{2,1,0:T(8,128)(2,1)S(1)}, u32[]{:S(2)}, u32[]{:S(2)}) async-start(bf16[16,208,128]{2,1,0:T(8,128)(2,1)} %truncate.1), calls=%async_computation | async-start | bytes 1703936 | tf_op jit(solution)/shard_map/all_to_all | solution.py:349
  16.2 5.8 %convolution_bitcast_fusion.one_ref = f32[512,512]{1,0:T(8,128)S(1)} fusion(bf16[4,32,32,512]{3,2,1,0:T(8,128)(2,1)} %field_ref.1), kind=kOutput, calls=%fused_computation | convolution fusion | flops 2147483648 | bytes 5242880 | tf_op jit(solution)/shard_map/dot_general | solution.py:352
  22.1 0.6 split.1
  22.8 1.5 %collective-permute-done.1.got_ref = bf16[4,2,128,128]{3,2,1,0:T(8,128)(2,1)S(1)} collective-permute-done((bf16[4,2,128,128]{3,2,1,0:T(8,128)(2,1)S(1)}, bf16[4,2,128,128]{3,2,1,0:T(8,128)(2,1)S(1)}, u32[]{:S(2)}, u32[]{:S(2)}) %collective-permute-start.1) | collective-permute-done | bytes 262176 | tf_op jit(solution)/shard_map/ppermute | solution.py:343
  24.4 1.7 %collective-permute-start.2 = (bf16[2,128,128]{2,1,0:T(8,128)(2,1)S(1)}, bf16[2,128,128]{2,1,0:T(8,128)(2,1)S(1)}, u32[]{:S(2)}, u32[]{:S(2)}) collective-permute-start(bf16[2,128,128]{2,1,0:T(8,128)(2,1)S(1)} %get-tuple-element.28), channel_id=1, source_target_pairs={{0,4},{1,5},{2,6},{3,7},{4,8},{5,9},{6,10},{7,11},{8,12},{9,13},{1... | collective-permute-start | bytes 196616 | tf_op jit(solution)/shard_map/ppermute | solution.py:343
  26.1 2.9 %collective-permute-start.3 = (bf16[2,128,128]{2,1,0:T(8,128)(2,1)S(1)}, bf16[2,128,128]{2,1,0:T(8,128)(2,1)S(1)}, u32[]{:S(2)}, u32[]{:S(2)}) collective-permute-start(bf16[2,128,128]{2,1,0:T(8,128)(2,1)S(1)} %get-tuple-element.29), channel_id=1, source_target_pairs={{0,8},{1,9},{2,10},{3,11},{4,12},{5,13},{6,14},{7,15},{8,0},{9,1},... | collective-permute-start | bytes 196616 | tf_op jit(solution)/shard_map/ppermute | solution.py:343
  29.0 1.3 %collective-permute-start.4 = (bf16[2,128,128]{2,1,0:T(8,128)(2,1)S(1)}, bf16[2,128,128]{2,1,0:T(8,128)(2,1)S(1)}, u32[]{:S(2)}, u32[]{:S(2)}) collective-permute-start(bf16[2,128,128]{2,1,0:T(8,128)(2,1)S(1)} %get-tuple-element.30), channel_id=1, source_target_pairs={{0,12},{1,13},{2,14},{3,15},{4,0},{5,1},{6,2},{7,3},{8,4},{9,5},{1... | collective-permute-start | bytes 196616 | tf_op jit(solution)/shard_map/ppermute | solution.py:343
  30.3 0.1 copy.7
  30.7 1.8 %collective-permute-done.3.refs_2_ = bf16[2,128,128]{2,1,0:T(8,128)(2,1)S(1)} collective-permute-done((bf16[2,128,128]{2,1,0:T(8,128)(2,1)S(1)}, bf16[2,128,128]{2,1,0:T(8,128)(2,1)S(1)}, u32[]{:S(2)}, u32[]{:S(2)}) %collective-permute-start.3) | collective-permute-done | bytes 65568 | tf_op jit(solution)/shard_map/ppermute | solution.py:343
  32.5 0.8 %collective-permute-done.4.refs_3_ = bf16[2,128,128]{2,1,0:T(8,128)(2,1)S(1)} collective-permute-done((bf16[2,128,128]{2,1,0:T(8,128)(2,1)S(1)}, bf16[2,128,128]{2,1,0:T(8,128)(2,1)S(1)}, u32[]{:S(2)}, u32[]{:S(2)}) %collective-permute-start.4) | collective-permute-done | bytes 65568 | tf_op jit(solution)/shard_map/ppermute | solution.py:343
  33.3 1.1 %collective-permute-start.5 = (bf16[128,128]{1,0:T(8,128)(2,1)S(1)}, bf16[128,128]{1,0:T(8,128)(2,1)S(1)}, u32[]{:S(2)}, u32[]{:S(2)}) collective-permute-start(bf16[128,128]{1,0:T(8,128)(2,1)S(1)} %get-tuple-element.32), channel_id=1, source_target_pairs={{0,2},{1,3},{2,0},{3,1},{4,6},{5,7},{6,4},{7,5},{8,10},{9,11},{10,... | collective-permute-start | bytes 98312 | tf_op jit(solution)/shard_map/ppermute | solution.py:343
  34.4 3.9 %all-to-all-done.whole_ref = bf16[16,208,128]{2,1,0:T(8,128)(2,1)S(1)} async-done(((bf16[16,208,128]{2,1,0:T(8,128)(2,1)}), bf16[16,208,128]{2,1,0:T(8,128)(2,1)S(1)}, u32[]{:S(2)}, u32[]{:S(2)}) %all-to-all-start) | async-done | bytes 852000 | tf_op jit(solution)/shard_map/all_to_all | solution.py:349
  38.2 0.5 gram_other.1.refs_0_
  38.7 0.6 collective-permute-start.6
  39.4 0.1 collective-permute-done.got_ref
  39.5 0.8 %core_other.1 = (bf16[8,112,128]{2,1,0:T(8,128)(2,1)S(1)}, bf16[128,768]{1,0:T(8,128)(2,1)S(1)}, bf16[128,768]{1,0:T(8,128)(2,1)S(1)}) custom-call(bf16[16,208,128]{2,1,0:T(8,128)(2,1)S(1)} %all-to-all-done.whole_ref, bf16[16,16,128]{2,1,0:T(8,128)(2,1)S(1)} %collective-permute-done.got_ref, bf16[768,256]{1,0:T(8,128)(2,1)S(1)} %select_bitcast_fusion.kron_ref, ...), custom_call_target="tpu_custom_call" | custom-call | tf_op jit(solution)/shard_map/core_other/pallas_call | solution.py:25
  40.3 0.2 collective-permute-start.7
  40.6 0.8 %own.1 = (bf16[8,128,128]{2,1,0:T(8,128)(2,1)S(1)}, f32[8,112,128]{2,1,0:T(8,128)S(1)}) custom-call(bf16[16,208,128]{2,1,0:T(8,128)(2,1)S(1)} %all-to-all-done.whole_ref, bf16[768,256]{1,0:T(8,128)(2,1)S(1)} %select_bitcast_fusion.kron_ref, bf16[128,768]{1,0:T(8,128)(2,1)S(1)} %get-tuple-element.33.high_ref, bf16[128,768]{1,0:T(8,128)(2,1)S(1)} %get-tuple-element.34.low_ref, ...), custom_call_target="tpu_custom_call" | custom-call | tf_op jit(solution)/shard_map/own/pallas_call | solution.py:25
  41.4 0.5 collective-permute-done.7.core_got_ref
  42.0 16.2 %all_to_all.15.in_ref = bf16[8,240,128]{2,1,0:T(8,128)(2,1)S(1)} all-to-all(bf16[8,240,128]{2,1,0:T(8,128)(2,1)S(1)} %pair.1), channel_id=1, replica_groups={{0,2,4,6,8,10,12,14},{1,3,5,7,9,11,13,15},{16,18,20,22,24,26,28,30},{17..., dimensions={0} | all-to-all | bytes 983040 | tf_op jit(solution)/shard_map/all_to_all | solution.py:372
  58.2 0.3 middle.1
  58.6 14.4 %all_to_all.16.refs_0_ = bf16[16,24,128]{2,1,0:T(8,128)(2,1)S(1)} all-to-all(bf16[16,24,128]{2,1,0:T(8,128)(2,1)S(1)} %middle.1), channel_id=1, replica_groups=mesh['gy'=16,'gz'=16] {'gy'}, dimensions={0} | all-to-all | bytes 196608 | tf_op jit(solution)/shard_map/all_to_all | solution.py:376
  72.9 0.9 %last.1 = (f32[2,512]{1,0:T(2,128)}, f32[2,512]{1,0:T(2,128)}, f32[6,6,4,96]{3,2,1,0:T(4,128)}) custom-call(bf16[16,24,128]{2,1,0:T(8,128)(2,1)S(1)} %all_to_all.16.refs_0_), custom_call_target="tpu_custom_call" | custom-call | tf_op jit(solution)/shard_map/last/pallas_call | solution.py:25
  (20 shorter events, 0.6 us)
Async XLA Ops:
  4.7 33.5 %all-to-all-start = ((bf16[16,208,128]{2,1,0:T(8,128)(2,1)}), bf16[16,208,128]{2,1,0:T(8,128)(2,1)S(1)}, u32[]{:S(2)}, u32[]{:S(2)}) async-start(bf16[16,208,128]{2,1,0:T(8,128)(2,1)} %truncate.1), calls=%async_computation | async-start | bytes 1703936 | tf_op jit(solution)/shard_map/all_to_all | solution.py:349
  16.2 14.1 %copy-start = (bf16[32,96]{1,0:T(8,128)(2,1)S(1)}, bf16[32,96]{1,0:T(8,128)(2,1)}, u32[]{:S(2)}) copy-start(bf16[32,96]{1,0:T(8,128)(2,1)} %param.7) | copy-start | bytes 18436
  22.7 1.6 %collective-permute-start.1 = (bf16[4,2,128,128]{3,2,1,0:T(8,128)(2,1)S(1)}, bf16[4,2,128,128]{3,2,1,0:T(8,128)(2,1)S(1)}, u32[]{:S(2)}, u32[]{:S(2)}) collective-permute-start(bf16[4,2,128,128]{3,2,1,0:T(8,128)(2,1)S(1)} %get-tuple-element.26), channel_id=1, source_target_pairs={{0,1},{1,0},{2,3},{3,2},{4,5},{5,4},{6,7},{7,6},{8,9},{9,8},{10,11... | collective-permute-start | bytes 786440 | tf_op jit(solution)/shard_map/ppermute | solution.py:343
  24.4 6.3 %collective-permute-start.2 = (bf16[2,128,128]{2,1,0:T(8,128)(2,1)S(1)}, bf16[2,128,128]{2,1,0:T(8,128)(2,1)S(1)}, u32[]{:S(2)}, u32[]{:S(2)}) collective-permute-start(bf16[2,128,128]{2,1,0:T(8,128)(2,1)S(1)} %get-tuple-element.28), channel_id=1, source_target_pairs={{0,4},{1,5},{2,6},{3,7},{4,8},{5,9},{6,10},{7,11},{8,12},{9,13},{1... | collective-permute-start | bytes 196616 | tf_op jit(solution)/shard_map/ppermute | solution.py:343
  26.1 6.4 %collective-permute-start.3 = (bf16[2,128,128]{2,1,0:T(8,128)(2,1)S(1)}, bf16[2,128,128]{2,1,0:T(8,128)(2,1)S(1)}, u32[]{:S(2)}, u32[]{:S(2)}) collective-permute-start(bf16[2,128,128]{2,1,0:T(8,128)(2,1)S(1)} %get-tuple-element.29), channel_id=1, source_target_pairs={{0,8},{1,9},{2,10},{3,11},{4,12},{5,13},{6,14},{7,15},{8,0},{9,1},... | collective-permute-start | bytes 196616 | tf_op jit(solution)/shard_map/ppermute | solution.py:343
  29.0 4.3 %collective-permute-start.4 = (bf16[2,128,128]{2,1,0:T(8,128)(2,1)S(1)}, bf16[2,128,128]{2,1,0:T(8,128)(2,1)S(1)}, u32[]{:S(2)}, u32[]{:S(2)}) collective-permute-start(bf16[2,128,128]{2,1,0:T(8,128)(2,1)S(1)} %get-tuple-element.30), channel_id=1, source_target_pairs={{0,12},{1,13},{2,14},{3,15},{4,0},{5,1},{6,2},{7,3},{8,4},{9,5},{1... | collective-permute-start | bytes 196616 | tf_op jit(solution)/shard_map/ppermute | solution.py:343
  33.3 6.1 %collective-permute-start.5 = (bf16[128,128]{1,0:T(8,128)(2,1)S(1)}, bf16[128,128]{1,0:T(8,128)(2,1)S(1)}, u32[]{:S(2)}, u32[]{:S(2)}) collective-permute-start(bf16[128,128]{1,0:T(8,128)(2,1)S(1)} %get-tuple-element.32), channel_id=1, source_target_pairs={{0,2},{1,3},{2,0},{3,1},{4,6},{5,7},{6,4},{7,5},{8,10},{9,11},{10,... | collective-permute-start | bytes 98312 | tf_op jit(solution)/shard_map/ppermute | solution.py:343
  38.2 1.3 %collective-permute-start = (bf16[16,16,128]{2,1,0:T(8,128)(2,1)S(1)}, bf16[16,16,128]{2,1,0:T(8,128)(2,1)S(1)}, u32[]{:S(2)}, u32[]{:S(2)}) collective-permute-start(bf16[16,16,128]{2,1,0:T(8,128)(2,1)S(1)} %slice.4), channel_id=1, source_target_pairs={{0,1},{1,0},{2,3},{3,2},{4,5},{5,4},{6,7},{7,6},{8,9},{9,8},{10,11... | collective-permute-start | bytes 196616 | tf_op jit(solution)/shard_map/ppermute | solution.py:343
  38.7 2.7 %collective-permute-start.6 = (bf16[8,128,128]{2,1,0:T(8,128)(2,1)S(1)}, bf16[8,128,128]{2,1,0:T(8,128)(2,1)S(1)}, u32[]{:S(2)}, u32[]{:S(2)}) collective-permute-start(bf16[8,128,128]{2,1,0:T(8,128)(2,1)S(1)} %gram_other.1.refs_0_), channel_id=1, source_target_pairs={{0,1},{1,0},{2,3},{3,2},{4,5},{5,4},{6,7},{7,6},{8,9},{9,8},{10,11... | collective-permute-start | bytes 786440 | tf_op jit(solution)/shard_map/ppermute | solution.py:343
  40.3 1.6 %collective-permute-start.7 = (bf16[8,112,128]{2,1,0:T(8,128)(2,1)S(1)}, bf16[8,112,128]{2,1,0:T(8,128)(2,1)S(1)}, u32[]{:S(2)}, u32[]{:S(2)}) collective-permute-start(bf16[8,112,128]{2,1,0:T(8,128)(2,1)S(1)} %get-tuple-element.35.after_ref), channel_id=1, source_target_pairs={{0,1},{1,0},{2,3},{3,2},{4,5},{5,4},{6,7},{7,6},{8,9},{9,8},{10,11... | collective-permute-start | bytes 688136 | tf_op jit(solution)/shard_map/ppermute | solution.py:343

commit v6 on v5

--- a/solution.py
+++ b/solution.py
@@ -286,8 +286,31 @@
 )
 
 
-def last_kernel(scale_one, scale_two, in_ref, one_ref, two_ref, core_ref, turned, ordered, core):
+def last_kernel(scale_one, scale_two, in_ref, one_ref, two_ref, core_ref, *scratch):
+    turned, ordered, core, one_out, two_out, core_out, sems = scratch
     got = in_ref[...].astype(F32)
+    lane = lax.broadcasted_iota(jnp.int32, (8, 128), 1)
+    row = lax.broadcasted_iota(jnp.int32, (8, 128), 0)
+    for v in range(4):
+        blocks = [got[v * 4 + g, 16:24] for g in range(4)]
+        for t in range(6):
+            ranks = jnp.zeros((8, 128), F32)
+            for g in range(4):
+                shift = (24 * (g - t)) % 128
+                moved = pltpu.roll(blocks[g], shift, 1) if shift else blocks[g]
+                if t == 5:
+                    rest = jnp.zeros((8, 128), F32)
+                    for s in range(6):
+                        turn = pltpu.roll(blocks[g], (24 * g + 8 - 16 * s) % 128, 1)
+                        rest = jnp.where(row == s, turn[6:7], rest)
+                    moved = jnp.where(lane < 24 * g + 8, moved, rest)
+                ranks = jnp.where((lane >= 24 * g) & (lane < 24 * g + 24), moved, ranks)
+            core[pl.ds(t * 4 + v, 8, stride=24), :] = ranks
+    for s in range(6):
+        for t in range(6):
+            core_out[s, t] = core[(s * 6 + t) * 4 : (s * 6 + t) * 4 + 4, 0:96]
+    copies = [pltpu.make_async_copy(core_out, core_ref, sems.at[0])]
+    copies[0].start()
     total = got[0, 0:16]
     for source in range(1, 16):
         total = total + got[source, 0:16]
@@ -300,37 +323,24 @@
     for e in range(2):
         for c in range(4):
             lanes = slice(c * 128, (c + 1) * 128)
-            one_ref[e : e + 1, lanes] = total[e * 4 + c : e * 4 + c + 1] * scale_one
-            two_ref[e : e + 1, lanes] = two[e * 4 + c : e * 4 + c + 1] * scale_two
-    lane = lax.broadcasted_iota(jnp.int32, (8, 128), 1)
-    row = lax.broadcasted_iota(jnp.int32, (8, 128), 0)
-    for v in range(4):
-        blocks = [got[v * 4 + g, 16:24] for g in range(4)]
-        for t in range(6):
-            ranks = jnp.zeros((8, 128), F32)
-            for g in range(4):
-                shift = (24 * (g - t)) % 128
-                moved = pltpu.roll(blocks[g], shift, 1) if shift else blocks[g]
-                if t == 5:
-                    rest = jnp.zeros((8, 128), F32)
-                    for s in range(6):
-                        turned = pltpu.roll(blocks[g], (24 * g + 8 - 16 * s) % 128, 1)
-                        rest = jnp.where(row == s, turned[6:7], rest)
-                    moved = jnp.where(lane < 24 * g + 8, moved, rest)
-                ranks = jnp.where((lane >= 24 * g) & (lane < 24 * g + 24), moved, ranks)
-            core[pl.ds(t * 4 + v, 8, stride=24), :] = ranks
-    for s in range(6):
-        for t in range(6):
-            core_ref[s, t] = core[(s * 6 + t) * 4 : (s * 6 + t) * 4 + 4, 0:96]
+            one_out[e : e + 1, lanes] = total[e * 4 + c : e * 4 + c + 1] * scale_one
+            two_out[e : e + 1, lanes] = two[e * 4 + c : e * 4 + c + 1] * scale_two
+    for held, out_ref in ((one_out, one_ref), (two_out, two_ref)):
+        copies.append(pltpu.make_async_copy(held, out_ref, sems.at[len(copies)]))
+        copies[-1].start()
+    for copy in copies:
+        copy.wait()
 
 
 def last(received, scale_one, scale_two):
     def body(*refs):
         last_kernel(scale_one, scale_two, *refs)
 
-    outs = (shape((2, 512), F32), shape((2, 512), F32), shape((6, 6, 4, 96), F32))
+    outs = ((2, 512), (2, 512), (6, 6, 4, 96))
     scratch = [pltpu.VMEM((rows, 128), F32) for rows in (128, 128, 192)]
-    return call(body, outs, scratch, name="last")(received)
+    scratch += [pltpu.VMEM(dims, F32) for dims in outs] + [pltpu.SemaphoreType.DMA((3,))]
+    outs = tuple(shape(dims, F32) for dims in outs)
+    return call(body, outs, scratch, out_specs=(HBM,) * 3, name="last")(received)
 
 
 def along_gz(y, z_lo, core):

time: 74.1 us -> 74.1 us (level)
  no operation moved by 1% of the time
where the time goes in v6:
time: 74.1 us; the launch traced here: 73.8 us
  blocking collectives  30.6 us (41%)
  starting transfers between devices  19.4 us (26%)
  waiting for transfers between devices  8.48 us (11%)
  Pallas kernels  8.27 us (11%)
  matrix products  5.82 us (8%)
  between operations  0.78 us (1%)
    all_to_all x1, blocking collectives, shards(): lax.all_to_all(summed, 'gz', split_axis=0, concat_axis=0, tiled=True, axi...  16.2 us
    all_to_all x1, blocking collectives, shards(): cut = lax.all_to_all(cut, 'gy', split_axis=0, concat_axis=0, tiled=True)  14.4 us
    all_to_all x1, starting transfers between devices, shards(): whole = lax.all_to_all(sent, 'gy', split_axis=0, concat_axis=0, tiled=True)  11.5 us
    pallas_call x10, Pallas kernels, call(): pl.pallas_call(kernel, out_shape=outs, in_specs=[VMEM] * len(args) if spe...  8.27 us
    ppermute x8, starting transfers between devices, send(): return lax.ppermute(block, 'gz', along_gz(y, z_lo, core))  7.93 us
    dot_general x1, matrix products, shards(): one = jnp.dot(flattened.T, flattened, preferred_element_type=F32)  5.82 us
    ppermute x8, waiting for transfers between devices, send(): return lax.ppermute(block, 'gz', along_gz(y, z_lo, core))  4.62 us
    all_to_all x1, waiting for transfers between devices, shards(): whole = lax.all_to_all(sent, 'gy', split_axis=0, concat_axis=0, tiled=True)  3.85 us
  transfers between devices with their start and end apart: 9, of which 6 were waited for; matrix products, arithmetic and copies ran while one was open for 8% of the time, Pallas kernels for 4%

profile of v6, /device:TPU:2, one launch (start us, length us, event | category | flops | bytes accessed | tf_op | source)
XLA Modules:
  0.0 73.8 jit_solution(7078699848733454388)
XLA Ops:
  0.6 4.1 %truncate.1 = bf16[16,208,128]{2,1,0:T(8,128)(2,1)} custom-call(bf16[96,512]{1,0:T(8,128)(2,1)} %bitcast.16, bf16[32,96]{1,0:T(8,128)(2,1)} %b2_ref.1, bf16[4,32,32,512]{3,2,1,0:T(8,128)(2,1)} %field_ref.1), custom_call_target="tpu_custom_call" | custom-call | tf_op jit(solution)/shard_map/truncate/pallas_call | solution.py:25
  4.7 11.5 %all-to-all-start = ((bf16[16,208,128]{2,1,0:T(8,128)(2,1)}), bf16[16,208,128]{2,1,0:T(8,128)(2,1)S(1)}, u32[]{:S(2)}, u32[]{:S(2)}) async-start(bf16[16,208,128]{2,1,0:T(8,128)(2,1)} %truncate.1), calls=%async_computation | async-start | bytes 1703936 | tf_op jit(solution)/shard_map/all_to_all | solution.py:359
  16.2 5.8 %convolution_bitcast_fusion.one_ref = f32[512,512]{1,0:T(8,128)S(1)} fusion(bf16[4,32,32,512]{3,2,1,0:T(8,128)(2,1)} %field_ref.1), kind=kOutput, calls=%fused_computation | convolution fusion | flops 2147483648 | bytes 5242880 | tf_op jit(solution)/shard_map/dot_general | solution.py:362
  22.1 0.6 split.1
  22.8 1.5 %collective-permute-done.1.got_ref = bf16[4,2,128,128]{3,2,1,0:T(8,128)(2,1)S(1)} collective-permute-done((bf16[4,2,128,128]{3,2,1,0:T(8,128)(2,1)S(1)}, bf16[4,2,128,128]{3,2,1,0:T(8,128)(2,1)S(1)}, u32[]{:S(2)}, u32[]{:S(2)}) %collective-permute-start.1) | collective-permute-done | bytes 262176 | tf_op jit(solution)/shard_map/ppermute | solution.py:353
  24.4 1.7 %collective-permute-start.2 = (bf16[2,128,128]{2,1,0:T(8,128)(2,1)S(1)}, bf16[2,128,128]{2,1,0:T(8,128)(2,1)S(1)}, u32[]{:S(2)}, u32[]{:S(2)}) collective-permute-start(bf16[2,128,128]{2,1,0:T(8,128)(2,1)S(1)} %get-tuple-element.28), channel_id=1, source_target_pairs={{0,4},{1,5},{2,6},{3,7},{4,8},{5,9},{6,10},{7,11},{8,12},{9,13},{1... | collective-permute-start | bytes 196616 | tf_op jit(solution)/shard_map/ppermute | solution.py:353
  26.1 2.9 %collective-permute-start.3 = (bf16[2,128,128]{2,1,0:T(8,128)(2,1)S(1)}, bf16[2,128,128]{2,1,0:T(8,128)(2,1)S(1)}, u32[]{:S(2)}, u32[]{:S(2)}) collective-permute-start(bf16[2,128,128]{2,1,0:T(8,128)(2,1)S(1)} %get-tuple-element.29), channel_id=1, source_target_pairs={{0,8},{1,9},{2,10},{3,11},{4,12},{5,13},{6,14},{7,15},{8,0},{9,1},... | collective-permute-start | bytes 196616 | tf_op jit(solution)/shard_map/ppermute | solution.py:353
  29.0 1.3 %collective-permute-start.4 = (bf16[2,128,128]{2,1,0:T(8,128)(2,1)S(1)}, bf16[2,128,128]{2,1,0:T(8,128)(2,1)S(1)}, u32[]{:S(2)}, u32[]{:S(2)}) collective-permute-start(bf16[2,128,128]{2,1,0:T(8,128)(2,1)S(1)} %get-tuple-element.30), channel_id=1, source_target_pairs={{0,12},{1,13},{2,14},{3,15},{4,0},{5,1},{6,2},{7,3},{8,4},{9,5},{1... | collective-permute-start | bytes 196616 | tf_op jit(solution)/shard_map/ppermute | solution.py:353
  30.3 0.1 copy.7
  30.7 1.8 %collective-permute-done.3.refs_2_ = bf16[2,128,128]{2,1,0:T(8,128)(2,1)S(1)} collective-permute-done((bf16[2,128,128]{2,1,0:T(8,128)(2,1)S(1)}, bf16[2,128,128]{2,1,0:T(8,128)(2,1)S(1)}, u32[]{:S(2)}, u32[]{:S(2)}) %collective-permute-start.3) | collective-permute-done | bytes 65568 | tf_op jit(solution)/shard_map/ppermute | solution.py:353
  32.5 0.8 %collective-permute-done.4.refs_3_ = bf16[2,128,128]{2,1,0:T(8,128)(2,1)S(1)} collective-permute-done((bf16[2,128,128]{2,1,0:T(8,128)(2,1)S(1)}, bf16[2,128,128]{2,1,0:T(8,128)(2,1)S(1)}, u32[]{:S(2)}, u32[]{:S(2)}) %collective-permute-start.4) | collective-permute-done | bytes 65568 | tf_op jit(solution)/shard_map/ppermute | solution.py:353
  33.3 1.1 %collective-permute-start.5 = (bf16[128,128]{1,0:T(8,128)(2,1)S(1)}, bf16[128,128]{1,0:T(8,128)(2,1)S(1)}, u32[]{:S(2)}, u32[]{:S(2)}) collective-permute-start(bf16[128,128]{1,0:T(8,128)(2,1)S(1)} %get-tuple-element.32), channel_id=1, source_target_pairs={{0,2},{1,3},{2,0},{3,1},{4,6},{5,7},{6,4},{7,5},{8,10},{9,11},{10,... | collective-permute-start | bytes 98312 | tf_op jit(solution)/shard_map/ppermute | solution.py:353
  34.4 3.9 %all-to-all-done.whole_ref = bf16[16,208,128]{2,1,0:T(8,128)(2,1)S(1)} async-done(((bf16[16,208,128]{2,1,0:T(8,128)(2,1)}), bf16[16,208,128]{2,1,0:T(8,128)(2,1)S(1)}, u32[]{:S(2)}, u32[]{:S(2)}) %all-to-all-start) | async-done | bytes 852000 | tf_op jit(solution)/shard_map/all_to_all | solution.py:359
  38.2 0.5 gram_other.1.refs_0_
  38.7 0.6 collective-permute-start.6
  39.4 0.1 collective-permute-done.got_ref
  39.5 0.8 %core_other.1 = (bf16[8,112,128]{2,1,0:T(8,128)(2,1)S(1)}, bf16[128,768]{1,0:T(8,128)(2,1)S(1)}, bf16[128,768]{1,0:T(8,128)(2,1)S(1)}) custom-call(bf16[16,208,128]{2,1,0:T(8,128)(2,1)S(1)} %all-to-all-done.whole_ref, bf16[16,16,128]{2,1,0:T(8,128)(2,1)S(1)} %collective-permute-done.got_ref, bf16[768,256]{1,0:T(8,128)(2,1)S(1)} %select_bitcast_fusion.kron_ref, ...), custom_call_target="tpu_custom_call" | custom-call | tf_op jit(solution)/shard_map/core_other/pallas_call | solution.py:25
  40.3 0.2 collective-permute-start.7
  40.6 0.8 %own.1 = (bf16[8,128,128]{2,1,0:T(8,128)(2,1)S(1)}, f32[8,112,128]{2,1,0:T(8,128)S(1)}) custom-call(bf16[16,208,128]{2,1,0:T(8,128)(2,1)S(1)} %all-to-all-done.whole_ref, bf16[768,256]{1,0:T(8,128)(2,1)S(1)} %select_bitcast_fusion.kron_ref, bf16[128,768]{1,0:T(8,128)(2,1)S(1)} %get-tuple-element.33.high_ref, bf16[128,768]{1,0:T(8,128)(2,1)S(1)} %get-tuple-element.34.low_ref, ...), custom_call_target="tpu_custom_call" | custom-call | tf_op jit(solution)/shard_map/own/pallas_call | solution.py:25
  41.4 0.5 collective-permute-done.7.core_got_ref
  42.0 16.2 %all_to_all.15.in_ref = bf16[8,240,128]{2,1,0:T(8,128)(2,1)S(1)} all-to-all(bf16[8,240,128]{2,1,0:T(8,128)(2,1)S(1)} %pair.1), channel_id=1, replica_groups={{0,2,4,6,8,10,12,14},{1,3,5,7,9,11,13,15},{16,18,20,22,24,26,28,30},{17..., dimensions={0} | all-to-all | bytes 983040 | tf_op jit(solution)/shard_map/all_to_all | solution.py:382
  58.2 0.3 middle.1
  58.6 14.4 %all_to_all.16.refs_0_ = bf16[16,24,128]{2,1,0:T(8,128)(2,1)S(1)} all-to-all(bf16[16,24,128]{2,1,0:T(8,128)(2,1)S(1)} %middle.1), channel_id=1, replica_groups=mesh['gy'=16,'gz'=16] {'gy'}, dimensions={0} | all-to-all | bytes 196608 | tf_op jit(solution)/shard_map/all_to_all | solution.py:386
  72.9 0.9 %last.1 = (f32[2,512]{1,0:T(2,128)}, f32[2,512]{1,0:T(2,128)}, f32[6,6,4,96]{3,2,1,0:T(4,128)}) custom-call(bf16[16,24,128]{2,1,0:T(8,128)(2,1)S(1)} %all_to_all.16.refs_0_), custom_call_target="tpu_custom_call" | custom-call | tf_op jit(solution)/shard_map/last/pallas_call | solution.py:25
  (20 shorter events, 0.6 us)
Async XLA Ops:
  4.7 33.5 %all-to-all-start = ((bf16[16,208,128]{2,1,0:T(8,128)(2,1)}), bf16[16,208,128]{2,1,0:T(8,128)(2,1)S(1)}, u32[]{:S(2)}, u32[]{:S(2)}) async-start(bf16[16,208,128]{2,1,0:T(8,128)(2,1)} %truncate.1), calls=%async_computation | async-start | bytes 1703936 | tf_op jit(solution)/shard_map/all_to_all | solution.py:359
  16.2 14.1 %copy-start = (bf16[32,96]{1,0:T(8,128)(2,1)S(1)}, bf16[32,96]{1,0:T(8,128)(2,1)}, u32[]{:S(2)}) copy-start(bf16[32,96]{1,0:T(8,128)(2,1)} %param.7) | copy-start | bytes 18436
  22.7 1.6 %collective-permute-start.1 = (bf16[4,2,128,128]{3,2,1,0:T(8,128)(2,1)S(1)}, bf16[4,2,128,128]{3,2,1,0:T(8,128)(2,1)S(1)}, u32[]{:S(2)}, u32[]{:S(2)}) collective-permute-start(bf16[4,2,128,128]{3,2,1,0:T(8,128)(2,1)S(1)} %get-tuple-element.26), channel_id=1, source_target_pairs={{0,1},{1,0},{2,3},{3,2},{4,5},{5,4},{6,7},{7,6},{8,9},{9,8},{10,11... | collective-permute-start | bytes 786440 | tf_op jit(solution)/shard_map/ppermute | solution.py:353
  24.4 6.3 %collective-permute-start.2 = (bf16[2,128,128]{2,1,0:T(8,128)(2,1)S(1)}, bf16[2,128,128]{2,1,0:T(8,128)(2,1)S(1)}, u32[]{:S(2)}, u32[]{:S(2)}) collective-permute-start(bf16[2,128,128]{2,1,0:T(8,128)(2,1)S(1)} %get-tuple-element.28), channel_id=1, source_target_pairs={{0,4},{1,5},{2,6},{3,7},{4,8},{5,9},{6,10},{7,11},{8,12},{9,13},{1... | collective-permute-start | bytes 196616 | tf_op jit(solution)/shard_map/ppermute | solution.py:353
  26.1 6.4 %collective-permute-start.3 = (bf16[2,128,128]{2,1,0:T(8,128)(2,1)S(1)}, bf16[2,128,128]{2,1,0:T(8,128)(2,1)S(1)}, u32[]{:S(2)}, u32[]{:S(2)}) collective-permute-start(bf16[2,128,128]{2,1,0:T(8,128)(2,1)S(1)} %get-tuple-element.29), channel_id=1, source_target_pairs={{0,8},{1,9},{2,10},{3,11},{4,12},{5,13},{6,14},{7,15},{8,0},{9,1},... | collective-permute-start | bytes 196616 | tf_op jit(solution)/shard_map/ppermute | solution.py:353
  29.0 4.3 %collective-permute-start.4 = (bf16[2,128,128]{2,1,0:T(8,128)(2,1)S(1)}, bf16[2,128,128]{2,1,0:T(8,128)(2,1)S(1)}, u32[]{:S(2)}, u32[]{:S(2)}) collective-permute-start(bf16[2,128,128]{2,1,0:T(8,128)(2,1)S(1)} %get-tuple-element.30), channel_id=1, source_target_pairs={{0,12},{1,13},{2,14},{3,15},{4,0},{5,1},{6,2},{7,3},{8,4},{9,5},{1... | collective-permute-start | bytes 196616 | tf_op jit(solution)/shard_map/ppermute | solution.py:353
  33.3 6.1 %collective-permute-start.5 = (bf16[128,128]{1,0:T(8,128)(2,1)S(1)}, bf16[128,128]{1,0:T(8,128)(2,1)S(1)}, u32[]{:S(2)}, u32[]{:S(2)}) collective-permute-start(bf16[128,128]{1,0:T(8,128)(2,1)S(1)} %get-tuple-element.32), channel_id=1, source_target_pairs={{0,2},{1,3},{2,0},{3,1},{4,6},{5,7},{6,4},{7,5},{8,10},{9,11},{10,... | collective-permute-start | bytes 98312 | tf_op jit(solution)/shard_map/ppermute | solution.py:353
  38.2 1.3 %collective-permute-start = (bf16[16,16,128]{2,1,0:T(8,128)(2,1)S(1)}, bf16[16,16,128]{2,1,0:T(8,128)(2,1)S(1)}, u32[]{:S(2)}, u32[]{:S(2)}) collective-permute-start(bf16[16,16,128]{2,1,0:T(8,128)(2,1)S(1)} %slice.4), channel_id=1, source_target_pairs={{0,1},{1,0},{2,3},{3,2},{4,5},{5,4},{6,7},{7,6},{8,9},{9,8},{10,11... | collective-permute-start | bytes 196616 | tf_op jit(solution)/shard_map/ppermute | solution.py:353
  38.7 2.7 %collective-permute-start.6 = (bf16[8,128,128]{2,1,0:T(8,128)(2,1)S(1)}, bf16[8,128,128]{2,1,0:T(8,128)(2,1)S(1)}, u32[]{:S(2)}, u32[]{:S(2)}) collective-permute-start(bf16[8,128,128]{2,1,0:T(8,128)(2,1)S(1)} %gram_other.1.refs_0_), channel_id=1, source_target_pairs={{0,1},{1,0},{2,3},{3,2},{4,5},{5,4},{6,7},{7,6},{8,9},{9,8},{10,11... | collective-permute-start | bytes 786440 | tf_op jit(solution)/shard_map/ppermute | solution.py:353
  40.3 1.6 %collective-permute-start.7 = (bf16[8,112,128]{2,1,0:T(8,128)(2,1)S(1)}, bf16[8,112,128]{2,1,0:T(8,128)(2,1)S(1)}, u32[]{:S(2)}, u32[]{:S(2)}) collective-permute-start(bf16[8,112,128]{2,1,0:T(8,128)(2,1)S(1)} %get-tuple-element.35.after_ref), channel_id=1, source_target_pairs={{0,1},{1,0},{2,3},{3,2},{4,5},{5,4},{6,7},{7,6},{8,9},{9,8},{10,11... | collective-permute-start | bytes 688136 | tf_op jit(solution)/shard_map/ppermute | solution.py:353

commit v7 on v6

--- a/solution.py
+++ b/solution.py
@@ -160,13 +160,15 @@
         parts = [whole_ref[:, pl.ds(a * 32 + first, size), :] for a in range(6)]
         return jnp.concatenate([part.reshape(16 * size, 128) for part in parts], axis=1)
 
-    values = nt_dot(cells(pl.multiple_of(side * 16, 16), 16), cells(0, 32))
-    for c in range(4):
-        gram[c * 256 : (c + 1) * 256, :] = values[:, c * 128 : (c + 1) * 128]
-    for b in range(8):
-        for c in range(4):
-            rows = gram[pl.ds(c * 256 + b, 32, stride=8), :]
-            out_ref[b, c * 32 : c * 32 + 32, :] = rows.astype(BF16)
+    mine, whole = cells(pl.multiple_of(side * 16, 16), 16), cells(0, 32)
+    for half in range(2):
+        values = nt_dot(mine, whole[half * 256 : half * 256 + 256])
+        for c in range(half * 2, half * 2 + 2):
+            at = c % 2 * 128
+            gram[c * 256 : (c + 1) * 256, :] = values[:, at : at + 128]
+            for b in range(8):
+                rows = gram[pl.ds(c * 256 + b, 32, stride=8), :]
+                out_ref[b, c * 32 : c * 32 + 32, :] = rows.astype(BF16)
 
 
 def core_rows(kron_ref, high_ref, low_ref, side, out_ref):

time: 74.1 us -> 74.1 us (level)
  no operation moved by 1% of the time
where the time goes in v7:
time: 74.1 us; the launch traced here: 73.8 us
  blocking collectives  30.6 us (41%)
  starting transfers between devices  19.4 us (26%)
  waiting for transfers between devices  8.48 us (11%)
  Pallas kernels  8.27 us (11%)
  matrix products  5.82 us (8%)
  between operations  0.78 us (1%)
    all_to_all x1, blocking collectives, shards(): lax.all_to_all(summed, 'gz', split_axis=0, concat_axis=0, tiled=True, axi...  16.2 us
    all_to_all x1, blocking collectives, shards(): cut = lax.all_to_all(cut, 'gy', split_axis=0, concat_axis=0, tiled=True)  14.4 us
    all_to_all x1, starting transfers between devices, shards(): whole = lax.all_to_all(sent, 'gy', split_axis=0, concat_axis=0, tiled=True)  11.5 us
    pallas_call x10, Pallas kernels, call(): pl.pallas_call(kernel, out_shape=outs, in_specs=[VMEM] * len(args) if spe...  8.27 us
    ppermute x8, starting transfers between devices, send(): return lax.ppermute(block, 'gz', along_gz(y, z_lo, core))  7.93 us
    dot_general x1, matrix products, shards(): one = jnp.dot(flattened.T, flattened, preferred_element_type=F32)  5.82 us
    ppermute x8, waiting for transfers between devices, send(): return lax.ppermute(block, 'gz', along_gz(y, z_lo, core))  4.62 us
    all_to_all x1, waiting for transfers between devices, shards(): whole = lax.all_to_all(sent, 'gy', split_axis=0, concat_axis=0, tiled=True)  3.85 us
  transfers between devices with their start and end apart: 9, of which 6 were waited for; matrix products, arithmetic and copies ran while one was open for 8% of the time, Pallas kernels for 4%

profile of v7, /device:TPU:2, one launch (start us, length us, event | category | flops | bytes accessed | tf_op | source)
XLA Modules:
  0.0 73.8 jit_solution(7078699848733454388)
XLA Ops:
  0.6 4.1 %truncate.1 = bf16[16,208,128]{2,1,0:T(8,128)(2,1)} custom-call(bf16[96,512]{1,0:T(8,128)(2,1)} %bitcast.16, bf16[32,96]{1,0:T(8,128)(2,1)} %b2_ref.1, bf16[4,32,32,512]{3,2,1,0:T(8,128)(2,1)} %field_ref.1), custom_call_target="tpu_custom_call" | custom-call | tf_op jit(solution)/shard_map/truncate/pallas_call | solution.py:25
  4.7 11.5 %all-to-all-start = ((bf16[16,208,128]{2,1,0:T(8,128)(2,1)}), bf16[16,208,128]{2,1,0:T(8,128)(2,1)S(1)}, u32[]{:S(2)}, u32[]{:S(2)}) async-start(bf16[16,208,128]{2,1,0:T(8,128)(2,1)} %truncate.1), calls=%async_computation | async-start | bytes 1703936 | tf_op jit(solution)/shard_map/all_to_all | solution.py:361
  16.2 5.8 %convolution_bitcast_fusion.one_ref = f32[512,512]{1,0:T(8,128)S(1)} fusion(bf16[4,32,32,512]{3,2,1,0:T(8,128)(2,1)} %field_ref.1), kind=kOutput, calls=%fused_computation | convolution fusion | flops 2147483648 | bytes 5242880 | tf_op jit(solution)/shard_map/dot_general | solution.py:364
  22.1 0.6 split.1
  22.8 1.5 %collective-permute-done.1.got_ref = bf16[4,2,128,128]{3,2,1,0:T(8,128)(2,1)S(1)} collective-permute-done((bf16[4,2,128,128]{3,2,1,0:T(8,128)(2,1)S(1)}, bf16[4,2,128,128]{3,2,1,0:T(8,128)(2,1)S(1)}, u32[]{:S(2)}, u32[]{:S(2)}) %collective-permute-start.1) | collective-permute-done | bytes 262176 | tf_op jit(solution)/shard_map/ppermute | solution.py:355
  24.4 1.7 %collective-permute-start.2 = (bf16[2,128,128]{2,1,0:T(8,128)(2,1)S(1)}, bf16[2,128,128]{2,1,0:T(8,128)(2,1)S(1)}, u32[]{:S(2)}, u32[]{:S(2)}) collective-permute-start(bf16[2,128,128]{2,1,0:T(8,128)(2,1)S(1)} %get-tuple-element.28), channel_id=1, source_target_pairs={{0,4},{1,5},{2,6},{3,7},{4,8},{5,9},{6,10},{7,11},{8,12},{9,13},{1... | collective-permute-start | bytes 196616 | tf_op jit(solution)/shard_map/ppermute | solution.py:355
  26.1 2.9 %collective-permute-start.3 = (bf16[2,128,128]{2,1,0:T(8,128)(2,1)S(1)}, bf16[2,128,128]{2,1,0:T(8,128)(2,1)S(1)}, u32[]{:S(2)}, u32[]{:S(2)}) collective-permute-start(bf16[2,128,128]{2,1,0:T(8,128)(2,1)S(1)} %get-tuple-element.29), channel_id=1, source_target_pairs={{0,8},{1,9},{2,10},{3,11},{4,12},{5,13},{6,14},{7,15},{8,0},{9,1},... | collective-permute-start | bytes 196616 | tf_op jit(solution)/shard_map/ppermute | solution.py:355
  29.0 1.3 %collective-permute-start.4 = (bf16[2,128,128]{2,1,0:T(8,128)(2,1)S(1)}, bf16[2,128,128]{2,1,0:T(8,128)(2,1)S(1)}, u32[]{:S(2)}, u32[]{:S(2)}) collective-permute-start(bf16[2,128,128]{2,1,0:T(8,128)(2,1)S(1)} %get-tuple-element.30), channel_id=1, source_target_pairs={{0,12},{1,13},{2,14},{3,15},{4,0},{5,1},{6,2},{7,3},{8,4},{9,5},{1... | collective-permute-start | bytes 196616 | tf_op jit(solution)/shard_map/ppermute | solution.py:355
  30.3 0.1 copy.7
  30.7 1.8 %collective-permute-done.3.refs_2_ = bf16[2,128,128]{2,1,0:T(8,128)(2,1)S(1)} collective-permute-done((bf16[2,128,128]{2,1,0:T(8,128)(2,1)S(1)}, bf16[2,128,128]{2,1,0:T(8,128)(2,1)S(1)}, u32[]{:S(2)}, u32[]{:S(2)}) %collective-permute-start.3) | collective-permute-done | bytes 65568 | tf_op jit(solution)/shard_map/ppermute | solution.py:355
  32.5 0.8 %collective-permute-done.4.refs_3_ = bf16[2,128,128]{2,1,0:T(8,128)(2,1)S(1)} collective-permute-done((bf16[2,128,128]{2,1,0:T(8,128)(2,1)S(1)}, bf16[2,128,128]{2,1,0:T(8,128)(2,1)S(1)}, u32[]{:S(2)}, u32[]{:S(2)}) %collective-permute-start.4) | collective-permute-done | bytes 65568 | tf_op jit(solution)/shard_map/ppermute | solution.py:355
  33.3 1.1 %collective-permute-start.5 = (bf16[128,128]{1,0:T(8,128)(2,1)S(1)}, bf16[128,128]{1,0:T(8,128)(2,1)S(1)}, u32[]{:S(2)}, u32[]{:S(2)}) collective-permute-start(bf16[128,128]{1,0:T(8,128)(2,1)S(1)} %get-tuple-element.32), channel_id=1, source_target_pairs={{0,2},{1,3},{2,0},{3,1},{4,6},{5,7},{6,4},{7,5},{8,10},{9,11},{10,... | collective-permute-start | bytes 98312 | tf_op jit(solution)/shard_map/ppermute | solution.py:355
  34.4 3.9 %all-to-all-done.whole_ref = bf16[16,208,128]{2,1,0:T(8,128)(2,1)S(1)} async-done(((bf16[16,208,128]{2,1,0:T(8,128)(2,1)}), bf16[16,208,128]{2,1,0:T(8,128)(2,1)S(1)}, u32[]{:S(2)}, u32[]{:S(2)}) %all-to-all-start) | async-done | bytes 852000 | tf_op jit(solution)/shard_map/all_to_all | solution.py:361
  38.2 0.5 gram_other.1.refs_0_
  38.7 0.6 collective-permute-start.6
  39.4 0.1 collective-permute-done.got_ref
  39.5 0.8 %core_other.1 = (bf16[8,112,128]{2,1,0:T(8,128)(2,1)S(1)}, bf16[128,768]{1,0:T(8,128)(2,1)S(1)}, bf16[128,768]{1,0:T(8,128)(2,1)S(1)}) custom-call(bf16[16,208,128]{2,1,0:T(8,128)(2,1)S(1)} %all-to-all-done.whole_ref, bf16[16,16,128]{2,1,0:T(8,128)(2,1)S(1)} %collective-permute-done.got_ref, bf16[768,256]{1,0:T(8,128)(2,1)S(1)} %select_bitcast_fusion.kron_ref, ...), custom_call_target="tpu_custom_call" | custom-call | tf_op jit(solution)/shard_map/core_other/pallas_call | solution.py:25
  40.3 0.2 collective-permute-start.7
  40.6 0.8 %own.1 = (bf16[8,128,128]{2,1,0:T(8,128)(2,1)S(1)}, f32[8,112,128]{2,1,0:T(8,128)S(1)}) custom-call(bf16[16,208,128]{2,1,0:T(8,128)(2,1)S(1)} %all-to-all-done.whole_ref, bf16[768,256]{1,0:T(8,128)(2,1)S(1)} %select_bitcast_fusion.kron_ref, bf16[128,768]{1,0:T(8,128)(2,1)S(1)} %get-tuple-element.33.high_ref, bf16[128,768]{1,0:T(8,128)(2,1)S(1)} %get-tuple-element.34.low_ref, ...), custom_call_target="tpu_custom_call" | custom-call | tf_op jit(solution)/shard_map/own/pallas_call | solution.py:25
  41.4 0.5 collective-permute-done.7.core_got_ref
  42.0 16.2 %all_to_all.15.in_ref = bf16[8,240,128]{2,1,0:T(8,128)(2,1)S(1)} all-to-all(bf16[8,240,128]{2,1,0:T(8,128)(2,1)S(1)} %pair.1), channel_id=1, replica_groups={{0,2,4,6,8,10,12,14},{1,3,5,7,9,11,13,15},{16,18,20,22,24,26,28,30},{17..., dimensions={0} | all-to-all | bytes 983040 | tf_op jit(solution)/shard_map/all_to_all | solution.py:384
  58.2 0.3 middle.1
  58.6 14.4 %all_to_all.16.refs_0_ = bf16[16,24,128]{2,1,0:T(8,128)(2,1)S(1)} all-to-all(bf16[16,24,128]{2,1,0:T(8,128)(2,1)S(1)} %middle.1), channel_id=1, replica_groups=mesh['gy'=16,'gz'=16] {'gy'}, dimensions={0} | all-to-all | bytes 196608 | tf_op jit(solution)/shard_map/all_to_all | solution.py:388
  72.9 0.9 %last.1 = (f32[2,512]{1,0:T(2,128)}, f32[2,512]{1,0:T(2,128)}, f32[6,6,4,96]{3,2,1,0:T(4,128)}) custom-call(bf16[16,24,128]{2,1,0:T(8,128)(2,1)S(1)} %all_to_all.16.refs_0_), custom_call_target="tpu_custom_call" | custom-call | tf_op jit(solution)/shard_map/last/pallas_call | solution.py:25
  (20 shorter events, 0.6 us)
Async XLA Ops:
  4.7 33.5 %all-to-all-start = ((bf16[16,208,128]{2,1,0:T(8,128)(2,1)}), bf16[16,208,128]{2,1,0:T(8,128)(2,1)S(1)}, u32[]{:S(2)}, u32[]{:S(2)}) async-start(bf16[16,208,128]{2,1,0:T(8,128)(2,1)} %truncate.1), calls=%async_computation | async-start | bytes 1703936 | tf_op jit(solution)/shard_map/all_to_all | solution.py:361
  16.2 14.1 %copy-start = (bf16[32,96]{1,0:T(8,128)(2,1)S(1)}, bf16[32,96]{1,0:T(8,128)(2,1)}, u32[]{:S(2)}) copy-start(bf16[32,96]{1,0:T(8,128)(2,1)} %param.7) | copy-start | bytes 18436
  22.7 1.6 %collective-permute-start.1 = (bf16[4,2,128,128]{3,2,1,0:T(8,128)(2,1)S(1)}, bf16[4,2,128,128]{3,2,1,0:T(8,128)(2,1)S(1)}, u32[]{:S(2)}, u32[]{:S(2)}) collective-permute-start(bf16[4,2,128,128]{3,2,1,0:T(8,128)(2,1)S(1)} %get-tuple-element.26), channel_id=1, source_target_pairs={{0,1},{1,0},{2,3},{3,2},{4,5},{5,4},{6,7},{7,6},{8,9},{9,8},{10,11... | collective-permute-start | bytes 786440 | tf_op jit(solution)/shard_map/ppermute | solution.py:355
  24.4 6.3 %collective-permute-start.2 = (bf16[2,128,128]{2,1,0:T(8,128)(2,1)S(1)}, bf16[2,128,128]{2,1,0:T(8,128)(2,1)S(1)}, u32[]{:S(2)}, u32[]{:S(2)}) collective-permute-start(bf16[2,128,128]{2,1,0:T(8,128)(2,1)S(1)} %get-tuple-element.28), channel_id=1, source_target_pairs={{0,4},{1,5},{2,6},{3,7},{4,8},{5,9},{6,10},{7,11},{8,12},{9,13},{1... | collective-permute-start | bytes 196616 | tf_op jit(solution)/shard_map/ppermute | solution.py:355
  26.1 6.4 %collective-permute-start.3 = (bf16[2,128,128]{2,1,0:T(8,128)(2,1)S(1)}, bf16[2,128,128]{2,1,0:T(8,128)(2,1)S(1)}, u32[]{:S(2)}, u32[]{:S(2)}) collective-permute-start(bf16[2,128,128]{2,1,0:T(8,128)(2,1)S(1)} %get-tuple-element.29), channel_id=1, source_target_pairs={{0,8},{1,9},{2,10},{3,11},{4,12},{5,13},{6,14},{7,15},{8,0},{9,1},... | collective-permute-start | bytes 196616 | tf_op jit(solution)/shard_map/ppermute | solution.py:355
  29.0 4.3 %collective-permute-start.4 = (bf16[2,128,128]{2,1,0:T(8,128)(2,1)S(1)}, bf16[2,128,128]{2,1,0:T(8,128)(2,1)S(1)}, u32[]{:S(2)}, u32[]{:S(2)}) collective-permute-start(bf16[2,128,128]{2,1,0:T(8,128)(2,1)S(1)} %get-tuple-element.30), channel_id=1, source_target_pairs={{0,12},{1,13},{2,14},{3,15},{4,0},{5,1},{6,2},{7,3},{8,4},{9,5},{1... | collective-permute-start | bytes 196616 | tf_op jit(solution)/shard_map/ppermute | solution.py:355
  33.3 6.1 %collective-permute-start.5 = (bf16[128,128]{1,0:T(8,128)(2,1)S(1)}, bf16[128,128]{1,0:T(8,128)(2,1)S(1)}, u32[]{:S(2)}, u32[]{:S(2)}) collective-permute-start(bf16[128,128]{1,0:T(8,128)(2,1)S(1)} %get-tuple-element.32), channel_id=1, source_target_pairs={{0,2},{1,3},{2,0},{3,1},{4,6},{5,7},{6,4},{7,5},{8,10},{9,11},{10,... | collective-permute-start | bytes 98312 | tf_op jit(solution)/shard_map/ppermute | solution.py:355
  38.2 1.3 %collective-permute-start = (bf16[16,16,128]{2,1,0:T(8,128)(2,1)S(1)}, bf16[16,16,128]{2,1,0:T(8,128)(2,1)S(1)}, u32[]{:S(2)}, u32[]{:S(2)}) collective-permute-start(bf16[16,16,128]{2,1,0:T(8,128)(2,1)S(1)} %slice.4), channel_id=1, source_target_pairs={{0,1},{1,0},{2,3},{3,2},{4,5},{5,4},{6,7},{7,6},{8,9},{9,8},{10,11... | collective-permute-start | bytes 196616 | tf_op jit(solution)/shard_map/ppermute | solution.py:355
  38.7 2.7 %collective-permute-start.6 = (bf16[8,128,128]{2,1,0:T(8,128)(2,1)S(1)}, bf16[8,128,128]{2,1,0:T(8,128)(2,1)S(1)}, u32[]{:S(2)}, u32[]{:S(2)}) collective-permute-start(bf16[8,128,128]{2,1,0:T(8,128)(2,1)S(1)} %gram_other.1.refs_0_), channel_id=1, source_target_pairs={{0,1},{1,0},{2,3},{3,2},{4,5},{5,4},{6,7},{7,6},{8,9},{9,8},{10,11... | collective-permute-start | bytes 786440 | tf_op jit(solution)/shard_map/ppermute | solution.py:355
  40.3 1.6 %collective-permute-start.7 = (bf16[8,112,128]{2,1,0:T(8,128)(2,1)S(1)}, bf16[8,112,128]{2,1,0:T(8,128)(2,1)S(1)}, u32[]{:S(2)}, u32[]{:S(2)}) collective-permute-start(bf16[8,112,128]{2,1,0:T(8,128)(2,1)S(1)} %get-tuple-element.35.after_ref), channel_id=1, source_target_pairs={{0,1},{1,0},{2,3},{3,2},{4,5},{5,4},{6,7},{7,6},{8,9},{9,8},{10,11... | collective-permute-start | bytes 688136 | tf_op jit(solution)/shard_map/ppermute | solution.py:355
